TPU v7x, 1024 devices: a whole 8x8x8 slice. The times are simulated.
1024 devices in a mesh: stn: 32 (over y_hi, x, core), chan: 8 (over z), tchunk: 4 (over y_lo).
Axes of the slice: x: 8, y: 8 (y_hi: 2, y_lo: 4; y = y_hi * 4 + y_lo), z: 8, core: 2. Of those that a mesh axis runs over, the one named last changes fastest.
Arguments:
- voltages: bfloat16 [512, 8, 512, 512], P('stn', 'chan', 'tchunk'), may hold values from -6 to 6
- weights: bfloat16 [512, 8, 2, 32, 256], P('stn', 'chan'), may hold values from -0.25 to 0.25
Outputs:
- visibilities: float32 [2, 8, 32, 512, 512], P(None, 'chan', 'stn', 'tchunk')
All inputs are finite; a program needn't handle non-finite values.
Results may differ from a plain program's by a relative error of at most 0.0029.
Values may be sent and summed in bfloat16 or wider, within the bound.
No kernel may reach another device: no remote copies, remote signals or barrier semaphores. Data moves between devices by JAX's collectives and lax.ppermute only.
A program may use at most 32 MiB of HBM per device.

v0:
```python
import jax
import jax.numpy as jnp
from jax import lax
from jax.sharding import PartitionSpec as P


def local(voltages, weights):
    stations = voltages.shape[0]
    channels = voltages.shape[1]
    samples = voltages.shape[2]
    beam_count = weights.shape[3]
    w_re = weights[:, :, 0]
    w_im = weights[:, :, 1]
    upper = jnp.concatenate([w_re, -w_im], axis=-1)
    lower = jnp.concatenate([w_im, w_re], axis=-1)
    matrix = jnp.concatenate([upper, lower], axis=2)
    formed = jnp.einsum("sftk,sfck->sftc", voltages, matrix, preferred_element_type=jnp.float32)
    formed = formed.astype(jnp.bfloat16).reshape(stations, channels, samples, 2, beam_count)
    formed = jnp.transpose(formed, (3, 1, 4, 0, 2))
    total_samples = samples * lax.axis_size("tchunk")
    turned = lax.all_to_all(formed, "stn", split_axis=2, concat_axis=3, tiled=True)
    all_stations = turned.shape[3]
    row_count = all_stations // lax.axis_size("tchunk")
    row_start = lax.axis_index("tchunk") * row_count
    piece = lax.all_gather(turned, "tchunk", axis=4, tiled=True)
    left = jnp.concatenate([piece[0], piece[1]], axis=-1)
    other = jnp.concatenate([piece[1], -piece[0]], axis=-1)
    left_rows = lax.dynamic_slice_in_dim(left, row_start, row_count, 2)
    other_rows = lax.dynamic_slice_in_dim(other, row_start, row_count, 2)
    vis_re = jnp.einsum("fbrk,fbsk->fbrs", left_rows, left, preferred_element_type=jnp.float32)
    vis_im = jnp.einsum("fbrk,fbsk->fbrs", other_rows, left, preferred_element_type=jnp.float32)
    result = jnp.stack([vis_re, vis_im])
    return result / total_samples


def solution(mesh):
    in_specs = (P("stn", "chan", "tchunk", None), P("stn", "chan", None, None, None))
    out_specs = P(None, "chan", "stn", "tchunk", None)
    return jax.shard_map(local, mesh=mesh, in_specs=in_specs, out_specs=out_specs, check_vma=False)
```

profile of v0, /device:TPU:1, one launch (start us, length us, event | category | flops | bytes accessed | tf_op | source)
XLA Modules:
  0.0 93.7 jit_solution(6335608997795907335)
XLA Ops:
  6.5 0.0 copy-start
  6.5 0.0 all-gather.2.cloned.1.call-start
  6.5 1.2 %slice_bitcast_fusion.2 = (bf16[16,1,32,256]{3,2,0,1:T(8,128)(2,1)S(1)}, bf16[16,1,32,256]{3,2,0,1:T(8,128)(2,1)S(1)}) fusion(bf16[16,1,2,32,256]{4,3,2,1,0:T(8,128)(2,1)} %param.3), kind=kLoop, calls=%fused_computation.26 | loop fusion | bytes 1048576 | tf_op jit(solution)/shard_map/squeeze | solution.py:13
  7.8 1.0 %fusion.25 = bf16[16,1,32,256]{3,2,0,1:T(8,128)(2,1)S(1)} fusion(bf16[16,1,2,32,256]{4,3,2,1,0:T(8,128)(2,1)} %param.3), kind=kLoop, calls=%fused_computation.33 | loop fusion | flops 131072 | bytes 524288 | tf_op jit(solution)/shard_map/neg | solution.py:14
  8.7 0.0 copy-done
  8.7 0.8 fusion.2
  9.6 0.2 copy.17
  9.8 32.7 %all_to_all.12 = bf16[2,1,32,16,128]{4,3,0,1,2:T(8,128)(2,1)S(1)} all-to-all(bf16[2,1,32,16,128]{4,3,0,1,2:T(8,128)(2,1)S(1)} %bitcast.49), channel_id=1, replica_groups=mesh['stn'=32,'chan'=8,'tchunk'=4] {'stn'}, dimensions={2} | all-to-all | bytes 524288 | tf_op jit(solution)/shard_map/all_to_all | solution.py:21
  42.5 0.7 copy.12
  43.2 0.0 all-gather.2.cloned.1.call-update
  43.2 39.5 %all-gather.2.cloned.1.call-done = bf16[2,1,1,512,512]{4,3,0,2,1:T(8,128)(2,1)} async-done(((bf16[2,1,1,512,128]{4,3,0,2,1:T(8,128)(2,1)}), bf16[2,1,1,512,512]{4,3,0,2,1:T(8,128)(2,1)}) %all-gather.2.cloned.1.call-update) | async-done | bytes 1048592 | tf_op jit(solution)/shard_map/all_gather | solution.py:25
  82.7 0.0 copy-start.1
  82.7 1.2 %slice_bitcast_fusion.1 = bf16[1,1,512,512]{3,2,1,0:T(8,128)(2,1)S(1)} fusion(bf16[2,1,1,512,512]{4,3,2,1,0:T(8,128)(2,1)} %bitcast.46), kind=kLoop, calls=%fused_computation.19 | loop fusion | bytes 1048576 | tf_op jit(solution)/shard_map/squeeze | solution.py:26
  83.9 1.1 %fusion.26 = bf16[1,1,512,512]{3,2,1,0:T(8,128)(2,1)S(1)} fusion(bf16[2,1,1,512,512]{4,3,2,1,0:T(8,128)(2,1)} %bitcast.47), kind=kLoop, calls=%fused_computation.34 | loop fusion | flops 262144 | bytes 1048576 | tf_op jit(solution)/shard_map/neg | solution.py:27
  85.0 0.0 copy-done.1
  85.1 0.5 convolution_bitcast_fusion.1
  85.5 0.5 convolution_bitcast_fusion
  86.0 0.8 maximum_multiply_fusion
  (1 shorter events, 0.0 us)
Async XLA Ops:
  6.5 2.2 %copy-start = (bf16[16,1,128,512]{3,2,1,0:T(8,128)(2,1)S(1)}, bf16[16,1,128,512]{3,2,1,0:T(8,128)(2,1)}, u32[]{:S(2)}) copy-start(bf16[16,1,128,512]{3,2,1,0:T(8,128)(2,1)} %param.2) | copy-start | bytes 6291460
  6.5 76.2 %all-gather.2.cloned.1.call-start = ((), (), s32[]{:S(2)}) async-start(), calls=%async_computation.1 | async-start | bytes 1310720 | tf_op jit(solution)/shard_map/all_gather | solution.py:25
  82.7 2.3 %copy-start.1 = (bf16[2,1,1,512,512]{4,3,0,2,1:T(8,128)(2,1)S(1)}, bf16[2,1,1,512,512]{4,3,0,2,1:T(8,128)(2,1)}, u32[]{:S(2)}) copy-start(bf16[2,1,1,512,512]{4,3,0,2,1:T(8,128)(2,1)} %all-gather.2.cloned.1.call-done) | copy-start | bytes 3145732
Sparse Core Ops, SparseCore 0:
  43.4 39.3 all-gather.1
where the time goes:
time: 93.9 us; the launch traced here: 93.7 us
  waiting for transfers between devices  39.5 us (42%)
  blocking collectives  32.7 us (35%)
  between operations  13.5 us (14%)
  local copies, waits for them, and re-layouts  3.32 us (4%)
  other arithmetic  2.89 us (3%)
  matrix products  1.77 us (2%)
    all_gather x1, waiting for transfers between devices, local(): piece = lax.all_gather(turned, 'tchunk', axis=4, tiled=True)  39.5 us
    all_to_all x1, blocking collectives, local(): lax.all_to_all(formed, 'stn', split_axis=2, concat_axis=3, tiled=True)  32.7 us
  transfers between devices with their start and end apart: 1, of which 1 were waited for; matrix products, arithmetic and copies ran while one was open for 0% of the time, Pallas kernels for 0%

commit v1 on v0

v1 whole, which is shorter than its diff:
```python
import jax
import jax.numpy as jnp
from jax import lax
from jax.experimental import pallas as pl
from jax.experimental.pallas import tpu as pltpu
from jax.sharding import PartitionSpec as P

NT_DIMS = (((1,), (1,)), ((), ()))


def form_beams(copies, volt_ref, wgt_ref, out_ref, held):
    stations, beam_count = wgt_ref.shape[0], wgt_ref.shape[2]
    for s in range(stations):
        w_re = wgt_ref[s, 0]
        w_im = wgt_ref[s, 1]
        upper = jnp.concatenate([w_re, -w_im], axis=-1)
        lower = jnp.concatenate([w_im, w_re], axis=-1)
        matrix = jnp.concatenate([upper, lower], axis=0)
        formed = lax.dot_general(matrix, volt_ref[s], NT_DIMS, preferred_element_type=jnp.float32)
        held[:, 0, s, :] = formed[:beam_count]
        held[:, 1, s, :] = formed[beam_count:]
    rounded = held[...].astype(jnp.bfloat16)
    for c in range(copies):
        out_ref[:, c] = rounded


def correlate(scale, row_ref, beams_ref, out_ref):
    groups, times = beams_ref.shape[0], beams_ref.shape[1]
    stations, samples = beams_ref.shape[3], beams_ref.shape[4]
    row_groups = out_ref.shape[1] // stations
    first = row_ref[0] * row_groups
    vis_re = vis_im = None
    for t in range(times):
        re = beams_ref[:, t, 0].reshape(groups * stations, samples)
        im = beams_ref[:, t, 1].reshape(groups * stations, samples)
        left = jnp.concatenate([re, im], axis=-1)
        row_re = beams_ref[pl.ds(first, row_groups), t, 0].reshape(row_groups * stations, samples)
        row_im = beams_ref[pl.ds(first, row_groups), t, 1].reshape(row_groups * stations, samples)
        left_rows = jnp.concatenate([row_re, row_im], axis=-1)
        other_rows = jnp.concatenate([row_im, -row_re], axis=-1)
        rows = jnp.concatenate([left_rows, other_rows], axis=0)
        part = lax.dot_general(rows, left, NT_DIMS, preferred_element_type=jnp.float32)
        vis_re = part if vis_re is None else vis_re + part
    out_ref[...] = (vis_re * scale).reshape(out_ref.shape)


def local(voltages, weights):
    stations, _, samples, width = voltages.shape
    beam_count = weights.shape[3]
    times = lax.axis_size("tchunk")
    groups = lax.axis_size("stn")
    vmem = pl.BlockSpec(memory_space=pltpu.VMEM)
    formed = pl.pallas_call(
        lambda *refs: form_beams(times, *refs),
        out_shape=jax.ShapeDtypeStruct((beam_count, times, 2, stations, samples), jnp.bfloat16),
        in_specs=[vmem, vmem],
        out_specs=vmem,
        scratch_shapes=[pltpu.VMEM((beam_count, 2, stations, samples), jnp.float32)],
        compiler_params=pltpu.CompilerParams(vmem_limit_bytes=16 * 2**20),
        name="form_beams",
    )(voltages.reshape(stations, samples, width), weights.reshape(stations, 2, beam_count, width // 2))
    formed = formed.reshape(groups * times, 2, stations, samples)
    turned = lax.all_to_all(formed, ("stn", "tchunk"), 0, 0, tiled=True)
    turned = turned.reshape(groups, times, 2, stations, samples)
    row = lax.axis_index("tchunk").astype(jnp.int32).reshape(1)
    all_stations = groups * stations
    result = pl.pallas_call(
        lambda *refs: correlate(1.0 / (samples * times), *refs),
        out_shape=jax.ShapeDtypeStruct((2, all_stations // times, all_stations), jnp.float32),
        in_specs=[pl.BlockSpec(memory_space=pltpu.SMEM), vmem],
        out_specs=vmem,
        compiler_params=pltpu.CompilerParams(vmem_limit_bytes=16 * 2**20),
        name="correlate",
    )(row, turned)
    return result[:, None, None]


def solution(mesh):
    in_specs = (P("stn", "chan", "tchunk", None), P("stn", "chan", None, None, None))
    out_specs = P(None, "chan", "stn", "tchunk", None)
    return jax.shard_map(local, mesh=mesh, in_specs=in_specs, out_specs=out_specs, check_vma=False)
```

time: 93.9 us -> 56.3 us (0.60)
  blocking collectives: 32.7 us -> 0 us
  starting transfers between devices: 0.01 us -> 19.4 us
  between operations: 13.5 us -> 0.02 us
  waiting for transfers between devices: 39.5 us -> 30.8 us
  Pallas kernels: 0 us -> 3.23 us
  other arithmetic: 2.89 us -> 0 us
  matrix products: 1.77 us -> 0 us
    all_gather x1 -> x0, waiting for transfers between devices: 39.5 us -> none  [local(): piece = lax.all_gather(turned, 'tchunk', axis=4, tiled=True)]
    all_to_all x1 -> x0, blocking collectives: 32.7 us -> none  [local(): lax.all_to_all(formed, 'stn', split_axis=2, concat_axis=3, tiled=True)]
    all_to_all x0 -> x1, waiting for transfers between devices: none -> 30.8 us  [local(): turned = lax.all_to_all(formed, ('stn', 'tchunk'), 0, 0, tiled=True)]
    all_to_all x0 -> x1, starting transfers between devices: none -> 19.4 us  [local(): turned = lax.all_to_all(formed, ('stn', 'tchunk'), 0, 0, tiled=True)]
    pallas_call x0 -> x2, Pallas kernels: none -> 3.23 us  [the longest x1 1.97 us: local(): pl.pallas_call(lambda *refs: form_beams(times, *refs), out_shape=jax.Shap...]
    unnamed x4, local copies, waits for them, and re-layouts: 0.01 us -> 2.63 us
    squeeze x3 -> x0, local copies, waits for them, and re-layouts: 2.42 us -> none  [the longest x1 1.22 us: local(): w_im = weights[:, :, 1]]
    neg x2 -> x0, other arithmetic: 2.06 us -> none  [the longest x1 1.08 us: local(): other = jnp.concatenate([piece[1], -piece[0]], axis=-1)]
where the time goes in v1:
time: 56.3 us; the launch traced here: 56.1 us
  waiting for transfers between devices  30.8 us (55%)
  starting transfers between devices  19.4 us (34%)
  Pallas kernels  3.23 us (6%)
  local copies, waits for them, and re-layouts  2.63 us (5%)
    all_to_all x1, waiting for transfers between devices, local(): turned = lax.all_to_all(formed, ('stn', 'tchunk'), 0, 0, tiled=True)  30.8 us
    all_to_all x1, starting transfers between devices, local(): turned = lax.all_to_all(formed, ('stn', 'tchunk'), 0, 0, tiled=True)  19.4 us
    unnamed x4, local copies, waits for them, and re-layouts  2.63 us
    pallas_call x1, Pallas kernels, local(): pl.pallas_call(lambda *refs: form_beams(times, *refs), out_shape=jax.Shap...  1.97 us
    pallas_call x1, Pallas kernels, local(): pl.pallas_call(lambda *refs: correlate(1.0 / (samples * times), *refs), o...  1.26 us
  transfers between devices with their start and end apart: 1, of which 1 were waited for; matrix products, arithmetic and copies ran while one was open for 0% of the time, Pallas kernels for 0%

profile of v1, /device:TPU:1, one launch (start us, length us, event | category | flops | bytes accessed | tf_op | source)
XLA Modules:
  0.0 56.1 jit_solution(1437813575753058670)
XLA Ops:
  0.0 0.0 copy-start
  0.0 1.6 %copy-done = bf16[16,1,128,512]{3,2,1,0:T(8,128)(2,1)S(1)} copy-done((bf16[16,1,128,512]{3,2,1,0:T(8,128)(2,1)S(1)}, bf16[16,1,128,512]{3,2,1,0:T(8,128)(2,1)}, u32[]{:S(2)}) %copy-start) | copy-done | bytes 2097176
  1.6 0.0 copy-start.1
  1.6 1.0 %copy-done.1 = bf16[16,1,2,32,256]{4,3,2,1,0:T(8,128)(2,1)S(1)} copy-done((bf16[16,1,2,32,256]{4,3,2,1,0:T(8,128)(2,1)S(1)}, bf16[16,1,2,32,256]{4,3,2,1,0:T(8,128)(2,1)}, u32[]{:S(2)}) %copy-start.1) | copy-done | bytes 524312
  2.6 2.0 %form_beams.1 = bf16[32,4,2,16,128]{4,3,2,1,0:T(8,128)(2,1)} custom-call(bf16[16,128,512]{2,1,0:T(8,128)(2,1)S(1)} %bitcast.9, bf16[16,2,32,256]{3,2,1,0:T(8,128)(2,1)S(1)} %bitcast.10), custom_call_target="tpu_custom_call" | custom-call | tf_op jit(solution)/shard_map/form_beams/pallas_call | solution.py:53
  4.6 19.4 %all-to-all-start = ((bf16[128,2,16,128]{3,2,1,0:T(8,128)(2,1)}), bf16[128,2,16,128]{3,2,1,0:T(8,128)(2,1)S(1)}, u32[]{:S(2)}, u32[]{:S(2)}) async-start(bf16[128,2,16,128]{3,2,1,0:T(8,128)(2,1)} %bitcast.3), calls=%async_computation | async-start | bytes 2097152 | tf_op jit(solution)/shard_map/all_to_all | solution.py:63
  24.0 30.8 %all-to-all-done = bf16[128,2,16,128]{3,2,1,0:T(8,128)(2,1)S(1)} async-done(((bf16[128,2,16,128]{3,2,1,0:T(8,128)(2,1)}), bf16[128,2,16,128]{3,2,1,0:T(8,128)(2,1)S(1)}, u32[]{:S(2)}, u32[]{:S(2)}) %all-to-all-start) | async-done | bytes 1048608 | tf_op jit(solution)/shard_map/all_to_all | solution.py:63
  54.8 1.3 %correlate.1 = f32[2,128,512]{2,1,0:T(8,128)} custom-call(s32[1]{0:T(128)} %bitcast.refs_0_, bf16[32,4,2,16,128]{4,3,2,1,0:T(8,128)(2,1)S(1)} %bitcast.8), custom_call_target="tpu_custom_call" | custom-call | tf_op jit(solution)/shard_map/correlate/pallas_call | solution.py:67
Async XLA Ops:
  0.0 1.6 %copy-start = (bf16[16,1,128,512]{3,2,1,0:T(8,128)(2,1)S(1)}, bf16[16,1,128,512]{3,2,1,0:T(8,128)(2,1)}, u32[]{:S(2)}) copy-start(bf16[16,1,128,512]{3,2,1,0:T(8,128)(2,1)} %param.2) | copy-start | bytes 6291460
  1.6 1.0 %copy-start.1 = (bf16[16,1,2,32,256]{4,3,2,1,0:T(8,128)(2,1)S(1)}, bf16[16,1,2,32,256]{4,3,2,1,0:T(8,128)(2,1)}, u32[]{:S(2)}) copy-start(bf16[16,1,2,32,256]{4,3,2,1,0:T(8,128)(2,1)} %param.3) | copy-start | bytes 1572868
  4.6 50.2 %all-to-all-start = ((bf16[128,2,16,128]{3,2,1,0:T(8,128)(2,1)}), bf16[128,2,16,128]{3,2,1,0:T(8,128)(2,1)S(1)}, u32[]{:S(2)}, u32[]{:S(2)}) async-start(bf16[128,2,16,128]{3,2,1,0:T(8,128)(2,1)} %bitcast.3), calls=%async_computation | async-start | bytes 2097152 | tf_op jit(solution)/shard_map/all_to_all | solution.py:63

commit v2 on v1

v2 whole, which is shorter than its diff:
```python
import jax
import jax.numpy as jnp
from jax import lax
from jax.experimental import pallas as pl
from jax.experimental.pallas import tpu as pltpu
from jax.sharding import PartitionSpec as P

NT_DIMS = (((1,), (1,)), ((), ()))


def form_beams(copies, pieces, volt_hbm, wgt_hbm, out_ref, volt_ref, wgt_ref, held, sems):
    stations, beam_count = wgt_ref.shape[0], wgt_ref.shape[2]
    step = stations // pieces
    loads = []
    for p in range(pieces):
        part = pl.ds(p * step, step)
        loads.append(
            (
                pltpu.make_async_copy(wgt_hbm.at[part], wgt_ref.at[part], sems.at[0, p]),
                pltpu.make_async_copy(volt_hbm.at[part], volt_ref.at[part], sems.at[1, p]),
            )
        )
    for pair in loads:
        for load in pair:
            load.start()
    for s in range(stations):
        if s % step == 0:
            for load in loads[s // step]:
                load.wait()
        w_re = wgt_ref[s, 0]
        w_im = wgt_ref[s, 1]
        upper = jnp.concatenate([w_re, -w_im], axis=-1)
        lower = jnp.concatenate([w_im, w_re], axis=-1)
        matrix = jnp.concatenate([upper, lower], axis=0)
        formed = lax.dot_general(matrix, volt_ref[s], NT_DIMS, preferred_element_type=jnp.float32)
        held[s] = formed.reshape(held.shape[1:])
    rounded = jnp.transpose(held[...], (2, 1, 0, 3)).astype(jnp.bfloat16)
    for c in range(copies):
        out_ref[:, c] = rounded


def correlate(scale, row_ref, beams_ref, out_ref):
    groups, times = beams_ref.shape[0], beams_ref.shape[1]
    stations, samples = beams_ref.shape[3], beams_ref.shape[4]
    row_groups = out_ref.shape[1] // stations
    first = row_ref[0] * row_groups
    total = None
    for t in range(times):
        re = beams_ref[:, t, 0].reshape(groups * stations, samples)
        im = beams_ref[:, t, 1].reshape(groups * stations, samples)
        left = jnp.concatenate([re, im], axis=-1)
        row_re = beams_ref[pl.ds(first, row_groups), t, 0].reshape(row_groups * stations, samples)
        row_im = beams_ref[pl.ds(first, row_groups), t, 1].reshape(row_groups * stations, samples)
        left_rows = jnp.concatenate([row_re, row_im], axis=-1)
        other_rows = jnp.concatenate([row_im, -row_re], axis=-1)
        rows = jnp.concatenate([left_rows, other_rows], axis=0)
        part = lax.dot_general(rows, left, NT_DIMS, preferred_element_type=jnp.float32)
        total = part if total is None else total + part
    out_ref[...] = (total * scale).reshape(out_ref.shape).astype(out_ref.dtype)


def correlate_rows(row, beams, rows, columns, scale, dtype, name):
    return pl.pallas_call(
        lambda *refs: correlate(scale, *refs),
        out_shape=jax.ShapeDtypeStruct((2, rows, columns), dtype),
        in_specs=[pl.BlockSpec(memory_space=pltpu.SMEM), pl.BlockSpec(memory_space=pltpu.VMEM)],
        out_specs=pl.BlockSpec(memory_space=pltpu.VMEM),
        compiler_params=pltpu.CompilerParams(vmem_limit_bytes=16 * 2**20),
        cost_estimate=pl.CostEstimate(flops=4 * rows * columns * 512, bytes_accessed=2**20, transcendentals=0),
        name=name,
    )(row, beams)


def local(voltages, weights):
    stations, _, samples, width = voltages.shape
    beam_count = weights.shape[3]
    times = lax.axis_size("tchunk")
    groups = lax.axis_size("stn")
    vmem = pl.BlockSpec(memory_space=pltpu.VMEM)
    pieces = 2 if stations % 2 == 0 else 1
    formed = pl.pallas_call(
        lambda *refs: form_beams(times // 2, pieces, *refs),
        out_shape=jax.ShapeDtypeStruct((beam_count, times // 2, 2, stations, samples), jnp.bfloat16),
        in_specs=[pl.BlockSpec(memory_space=pltpu.HBM)] * 2,
        out_specs=vmem,
        scratch_shapes=[
            pltpu.VMEM((stations, samples, width), jnp.bfloat16),
            pltpu.VMEM((stations, 2, beam_count, width // 2), jnp.bfloat16),
            pltpu.VMEM((stations, 2, beam_count, samples), jnp.float32),
            pltpu.SemaphoreType.DMA((2, pieces)),
        ],
        compiler_params=pltpu.CompilerParams(vmem_limit_bytes=16 * 2**20),
        name="form_beams",
    )(
        pltpu.with_memory_space_constraint(voltages.reshape(stations, samples, width), pltpu.HBM),
        pltpu.with_memory_space_constraint(weights.reshape(stations, 2, beam_count, width // 2), pltpu.HBM),
    )
    classes = [[g * times + t for g in range(groups) for t in range(c, times, 2)] for c in range(2)]
    formed = formed.reshape(groups * times // 2, 2, stations, samples)
    turned = lax.all_to_all(formed, ("stn", "tchunk"), 0, 0, axis_index_groups=classes, tiled=True)
    turned = turned.reshape(groups, times // 2, 2, stations, samples)
    row = lax.axis_index("tchunk").astype(jnp.int32).reshape(1)
    columns = groups * stations
    rows = columns // times
    scale = 1.0 / (samples * times)
    theirs = correlate_rows(row ^ 1, turned, rows, columns, scale, jnp.bfloat16, "correlate_theirs")
    arrived = lax.ppermute(theirs, "tchunk", [(t, t ^ 1) for t in range(times)])
    ours = correlate_rows(row, turned, rows, columns, scale, jnp.float32, "correlate_ours")
    return (ours + arrived.astype(jnp.float32))[:, None, None]


def solution(mesh):
    in_specs = (P("stn", "chan", "tchunk", None), P("stn", "chan", None, None, None))
    out_specs = P(None, "chan", "stn", "tchunk", None)
    return jax.shard_map(local, mesh=mesh, in_specs=in_specs, out_specs=out_specs, check_vma=False)
```

time: 56.3 us -> 53.6 us (0.952)
  local copies, waits for them, and re-layouts: 2.63 us -> 0 us
  waiting for transfers between devices: 30.8 us -> 28.5 us
  other arithmetic: 0 us -> 0.87 us
  starting transfers between devices: 19.4 us -> 20.2 us
  Pallas kernels: 3.23 us -> 3.8 us
    all_to_all x1, waiting for transfers between devices: 30.8 us -> 21.7 us  [local(): lax.all_to_all(formed, ('stn', 'tchunk'), 0, 0, axis_index_groups=classes...]
    ppermute x0 -> x1, waiting for transfers between devices: none -> 6.83 us  [local(): arrived = lax.ppermute(theirs, 'tchunk', [(t, t ^ 1) for t in range(times)])]
    unnamed x4 -> x0, local copies, waits for them, and re-layouts: 2.63 us -> none
    ppermute x0 -> x1, starting transfers between devices: none -> 1.92 us  [local(): arrived = lax.ppermute(theirs, 'tchunk', [(t, t ^ 1) for t in range(times)])]
    all_to_all x1, starting transfers between devices: 19.4 us -> 18.2 us  [local(): lax.all_to_all(formed, ('stn', 'tchunk'), 0, 0, axis_index_groups=classes...]
    broadcast_in_dim x0 -> x1, other arithmetic: none -> 0.87 us  [local(): return (ours + arrived.astype(jnp.float32))[:, None, None]]
    pallas_call x2 -> x3, Pallas kernels: 3.23 us -> 3.8 us  [the longest x1 3.13 us: local(): pl.pallas_call(lambda *refs: form_beams(times // 2, pieces, *refs), out_s...]
  transfers between devices with their start and end apart: 1 -> 2, of which waited for: 1 -> 2; matrix products, arithmetic and copies ran while one was open for 0% -> 0% of each run, Pallas kernels for 0% -> 1%
where the time goes in v2:
time: 53.6 us; the launch traced here: 53.4 us
  waiting for transfers between devices  28.5 us (53%)
  starting transfers between devices  20.2 us (38%)
  Pallas kernels  3.8 us (7%)
  other arithmetic  0.87 us (2%)
    all_to_all x1, waiting for transfers between devices, local(): lax.all_to_all(formed, ('stn', 'tchunk'), 0, 0, axis_index_groups=classes...  21.7 us
    all_to_all x1, starting transfers between devices, local(): lax.all_to_all(formed, ('stn', 'tchunk'), 0, 0, axis_index_groups=classes...  18.2 us
    ppermute x1, waiting for transfers between devices, local(): arrived = lax.ppermute(theirs, 'tchunk', [(t, t ^ 1) for t in range(times)])  6.83 us
    pallas_call x1, Pallas kernels, local(): pl.pallas_call(lambda *refs: form_beams(times // 2, pieces, *refs), out_s...  3.13 us
    ppermute x1, starting transfers between devices, local(): arrived = lax.ppermute(theirs, 'tchunk', [(t, t ^ 1) for t in range(times)])  1.92 us
  transfers between devices with their start and end apart: 2, of which 2 were waited for; matrix products, arithmetic and copies ran while one was open for 0% of the time, Pallas kernels for 1%

profile of v2, /device:TPU:1, one launch (start us, length us, event | category | flops | bytes accessed | tf_op | source)
XLA Modules:
  0.0 53.4 jit_solution(7604273761649696099)
XLA Ops:
  0.0 3.1 %form_beams.1 = bf16[32,2,2,16,128]{4,3,2,1,0:T(8,128)(2,1)} custom-call(bf16[16,128,512]{2,1,0:T(8,128)(2,1)} %bitcast.11, bf16[16,2,32,256]{3,2,1,0:T(8,128)(2,1)} %bitcast.12), custom_call_target="tpu_custom_call" | custom-call | tf_op jit(solution)/shard_map/form_beams/pallas_call | solution.py:81
  3.1 18.2 %all-to-all-start = ((bf16[64,2,16,128]{3,2,1,0:T(8,128)(2,1)}), bf16[64,2,16,128]{3,2,1,0:T(8,128)(2,1)S(1)}, u32[]{:S(2)}, u32[]{:S(2)}) async-start(bf16[64,2,16,128]{3,2,1,0:T(8,128)(2,1)} %bitcast.3), calls=%async_computation | async-start | bytes 1048576 | tf_op jit(solution)/shard_map/all_to_all | solution.py:100
  21.4 21.7 %all-to-all-done = bf16[64,2,16,128]{3,2,1,0:T(8,128)(2,1)S(1)} async-done(((bf16[64,2,16,128]{3,2,1,0:T(8,128)(2,1)}), bf16[64,2,16,128]{3,2,1,0:T(8,128)(2,1)S(1)}, u32[]{:S(2)}, u32[]{:S(2)}) %all-to-all-start) | async-done | bytes 524320 | tf_op jit(solution)/shard_map/all_to_all | solution.py:100
  43.1 0.3 correlate_theirs.1
  43.4 1.9 %collective-permute-start = (bf16[2,128,512]{2,1,0:T(8,128)(2,1)S(1)}, bf16[2,128,512]{2,1,0:T(8,128)(2,1)S(1)}, u32[]{:S(2)}, u32[]{:S(2)}) collective-permute-start(bf16[2,128,512]{2,1,0:T(8,128)(2,1)S(1)} %correlate_theirs.1), channel_id=1, source_target_pairs={{0,1},{1,0},{2,3},{3,2},{4,5},{5,4},{6,7},{7,6},{8,9},{9,8},{10,11... | collective-permute-start | bytes 786440 | tf_op jit(solution)/shard_map/ppermute | solution.py:107
  45.4 0.3 correlate_ours.1
  45.7 6.8 %collective-permute-done = bf16[2,128,512]{2,1,0:T(8,128)(2,1)S(1)} collective-permute-done((bf16[2,128,512]{2,1,0:T(8,128)(2,1)S(1)}, bf16[2,128,512]{2,1,0:T(8,128)(2,1)S(1)}, u32[]{:S(2)}, u32[]{:S(2)}) %collective-permute-start) | collective-permute-done | bytes 262176 | tf_op jit(solution)/shard_map/ppermute | solution.py:107
  52.5 0.9 %add_bitcast_fusion = f32[2,1,1,128,512]{4,3,2,1,0:T(8,128)} fusion(f32[2,128,512]{2,1,0:T(8,128)S(1)} %correlate_ours.1, bf16[2,128,512]{2,1,0:T(8,128)(2,1)S(1)} %collective-permute-done), kind=kLoop, calls=%fused_computation | loop fusion | flops 262144 | bytes 1310720 | tf_op jit(solution)/shard_map/broadcast_in_dim | solution.py:109
Async XLA Ops:
  3.1 39.9 %all-to-all-start = ((bf16[64,2,16,128]{3,2,1,0:T(8,128)(2,1)}), bf16[64,2,16,128]{3,2,1,0:T(8,128)(2,1)S(1)}, u32[]{:S(2)}, u32[]{:S(2)}) async-start(bf16[64,2,16,128]{3,2,1,0:T(8,128)(2,1)} %bitcast.3), calls=%async_computation | async-start | bytes 1048576 | tf_op jit(solution)/shard_map/all_to_all | solution.py:100
  43.4 9.1 %collective-permute-start = (bf16[2,128,512]{2,1,0:T(8,128)(2,1)S(1)}, bf16[2,128,512]{2,1,0:T(8,128)(2,1)S(1)}, u32[]{:S(2)}, u32[]{:S(2)}) collective-permute-start(bf16[2,128,512]{2,1,0:T(8,128)(2,1)S(1)} %correlate_theirs.1), channel_id=1, source_target_pairs={{0,1},{1,0},{2,3},{3,2},{4,5},{5,4},{6,7},{7,6},{8,9},{9,8},{10,11... | collective-permute-start | bytes 786440 | tf_op jit(solution)/shard_map/ppermute | solution.py:107

commit v3 on v2

--- a/solution.py
+++ b/solution.py
@@ -35,8 +35,9 @@
         formed = lax.dot_general(matrix, volt_ref[s], NT_DIMS, preferred_element_type=jnp.float32)
         held[s] = formed.reshape(held.shape[1:])
     rounded = jnp.transpose(held[...], (2, 1, 0, 3)).astype(jnp.bfloat16)
-    for c in range(copies):
-        out_ref[:, c] = rounded
+    for b in range(beam_count):
+        for c in range(copies):
+            out_ref[b ^ 1, c] = rounded[b]
 
 
 def correlate(scale, row_ref, beams_ref, out_ref):
@@ -46,11 +47,11 @@
     first = row_ref[0] * row_groups
     total = None
     for t in range(times):
-        re = beams_ref[:, t, 0].reshape(groups * stations, samples)
-        im = beams_ref[:, t, 1].reshape(groups * stations, samples)
+        re = jnp.concatenate([beams_ref[g ^ 1, t, 0] for g in range(groups)], axis=0)
+        im = jnp.concatenate([beams_ref[g ^ 1, t, 1] for g in range(groups)], axis=0)
         left = jnp.concatenate([re, im], axis=-1)
-        row_re = beams_ref[pl.ds(first, row_groups), t, 0].reshape(row_groups * stations, samples)
-        row_im = beams_ref[pl.ds(first, row_groups), t, 1].reshape(row_groups * stations, samples)
+        row_re = jnp.concatenate([beams_ref[first + (g ^ 1), t, 0] for g in range(row_groups)], axis=0)
+        row_im = jnp.concatenate([beams_ref[first + (g ^ 1), t, 1] for g in range(row_groups)], axis=0)
         left_rows = jnp.concatenate([row_re, row_im], axis=-1)
         other_rows = jnp.concatenate([row_im, -row_re], axis=-1)
         rows = jnp.concatenate([left_rows, other_rows], axis=0)
@@ -95,7 +96,7 @@
         pltpu.with_memory_space_constraint(voltages.reshape(stations, samples, width), pltpu.HBM),
         pltpu.with_memory_space_constraint(weights.reshape(stations, 2, beam_count, width // 2), pltpu.HBM),
     )
-    classes = [[g * times + t for g in range(groups) for t in range(c, times, 2)] for c in range(2)]
+    classes = [[(g ^ 1) * times + t for g in range(groups) for t in range(c, times, 2)] for c in range(2)]
     formed = formed.reshape(groups * times // 2, 2, stations, samples)
     turned = lax.all_to_all(formed, ("stn", "tchunk"), 0, 0, axis_index_groups=classes, tiled=True)
     turned = turned.reshape(groups, times // 2, 2, stations, samples)

time: 53.6 us -> 49.9 us (0.931)
  waiting for transfers between devices: 28.5 us -> 26.3 us
  starting transfers between devices: 20.2 us -> 18.4 us
    all_to_all x1, waiting for transfers between devices: 21.7 us -> 19.8 us  [local(): lax.all_to_all(formed, ('stn', 'tchunk'), 0, 0, axis_index_groups=classes...]
    all_to_all x1, starting transfers between devices: 18.2 us -> 16.5 us  [local(): lax.all_to_all(formed, ('stn', 'tchunk'), 0, 0, axis_index_groups=classes...]
where the time goes in v3:
time: 49.9 us; the launch traced here: 49.3 us
  waiting for transfers between devices  26.3 us (53%)
  starting transfers between devices  18.4 us (37%)
  Pallas kernels  3.79 us (8%)
  other arithmetic  0.87 us (2%)
    all_to_all x1, waiting for transfers between devices, local(): lax.all_to_all(formed, ('stn', 'tchunk'), 0, 0, axis_index_groups=classes...  19.8 us
    all_to_all x1, starting transfers between devices, local(): lax.all_to_all(formed, ('stn', 'tchunk'), 0, 0, axis_index_groups=classes...  16.5 us
    ppermute x1, waiting for transfers between devices, local(): arrived = lax.ppermute(theirs, 'tchunk', [(t, t ^ 1) for t in range(times)])  6.49 us
    pallas_call x1, Pallas kernels, local(): pl.pallas_call(lambda *refs: form_beams(times // 2, pieces, *refs), out_s...  3.13 us
    ppermute x1, starting transfers between devices, local(): arrived = lax.ppermute(theirs, 'tchunk', [(t, t ^ 1) for t in range(times)])  1.92 us
  transfers between devices with their start and end apart: 2, of which 2 were waited for; matrix products, arithmetic and copies ran while one was open for 0% of the time, Pallas kernels for 1%

profile of v3, /device:TPU:1, one launch (start us, length us, event | category | flops | bytes accessed | tf_op | source)
XLA Modules:
  0.0 49.3 jit_solution(3097114420242488518)
XLA Ops:
  0.0 3.1 %form_beams.1 = bf16[32,2,2,16,128]{4,3,2,1,0:T(8,128)(2,1)} custom-call(bf16[16,128,512]{2,1,0:T(8,128)(2,1)} %bitcast.11, bf16[16,2,32,256]{3,2,1,0:T(8,128)(2,1)} %bitcast.12), custom_call_target="tpu_custom_call" | custom-call | tf_op jit(solution)/shard_map/form_beams/pallas_call | solution.py:82
  3.1 16.5 %all-to-all-start = ((bf16[64,2,16,128]{3,2,1,0:T(8,128)(2,1)}), bf16[64,2,16,128]{3,2,1,0:T(8,128)(2,1)S(1)}, u32[]{:S(2)}, u32[]{:S(2)}) async-start(bf16[64,2,16,128]{3,2,1,0:T(8,128)(2,1)} %bitcast.3), calls=%async_computation | async-start | bytes 1048576 | tf_op jit(solution)/shard_map/all_to_all | solution.py:101
  19.6 19.8 %all-to-all-done = bf16[64,2,16,128]{3,2,1,0:T(8,128)(2,1)S(1)} async-done(((bf16[64,2,16,128]{3,2,1,0:T(8,128)(2,1)}), bf16[64,2,16,128]{3,2,1,0:T(8,128)(2,1)S(1)}, u32[]{:S(2)}, u32[]{:S(2)}) %all-to-all-start) | async-done | bytes 524320 | tf_op jit(solution)/shard_map/all_to_all | solution.py:101
  39.4 0.3 correlate_theirs.1
  39.7 1.9 %collective-permute-start = (bf16[2,128,512]{2,1,0:T(8,128)(2,1)S(1)}, bf16[2,128,512]{2,1,0:T(8,128)(2,1)S(1)}, u32[]{:S(2)}, u32[]{:S(2)}) collective-permute-start(bf16[2,128,512]{2,1,0:T(8,128)(2,1)S(1)} %correlate_theirs.1), channel_id=1, source_target_pairs={{0,1},{1,0},{2,3},{3,2},{4,5},{5,4},{6,7},{7,6},{8,9},{9,8},{10,11... | collective-permute-start | bytes 786440 | tf_op jit(solution)/shard_map/ppermute | solution.py:108
  41.6 0.3 correlate_ours.1
  42.0 6.5 %collective-permute-done = bf16[2,128,512]{2,1,0:T(8,128)(2,1)S(1)} collective-permute-done((bf16[2,128,512]{2,1,0:T(8,128)(2,1)S(1)}, bf16[2,128,512]{2,1,0:T(8,128)(2,1)S(1)}, u32[]{:S(2)}, u32[]{:S(2)}) %collective-permute-start) | collective-permute-done | bytes 262176 | tf_op jit(solution)/shard_map/ppermute | solution.py:108
  48.5 0.9 %add_bitcast_fusion = f32[2,1,1,128,512]{4,3,2,1,0:T(8,128)} fusion(f32[2,128,512]{2,1,0:T(8,128)S(1)} %correlate_ours.1, bf16[2,128,512]{2,1,0:T(8,128)(2,1)S(1)} %collective-permute-done), kind=kLoop, calls=%fused_computation | loop fusion | flops 262144 | bytes 1310720 | tf_op jit(solution)/shard_map/broadcast_in_dim | solution.py:110
Async XLA Ops:
  3.1 36.2 %all-to-all-start = ((bf16[64,2,16,128]{3,2,1,0:T(8,128)(2,1)}), bf16[64,2,16,128]{3,2,1,0:T(8,128)(2,1)S(1)}, u32[]{:S(2)}, u32[]{:S(2)}) async-start(bf16[64,2,16,128]{3,2,1,0:T(8,128)(2,1)} %bitcast.3), calls=%async_computation | async-start | bytes 1048576 | tf_op jit(solution)/shard_map/all_to_all | solution.py:101
  39.7 8.8 %collective-permute-start = (bf16[2,128,512]{2,1,0:T(8,128)(2,1)S(1)}, bf16[2,128,512]{2,1,0:T(8,128)(2,1)S(1)}, u32[]{:S(2)}, u32[]{:S(2)}) collective-permute-start(bf16[2,128,512]{2,1,0:T(8,128)(2,1)S(1)} %correlate_theirs.1), channel_id=1, source_target_pairs={{0,1},{1,0},{2,3},{3,2},{4,5},{5,4},{6,7},{7,6},{8,9},{9,8},{10,11... | collective-permute-start | bytes 786440 | tf_op jit(solution)/shard_map/ppermute | solution.py:108

commit v4 on v3

--- a/solution.py
+++ b/solution.py
@@ -40,36 +40,98 @@
             out_ref[b ^ 1, c] = rounded[b]
 
 
-def correlate(scale, row_ref, beams_ref, out_ref):
+def correlate(scale, packed, row_ref, beams_ref, *out_refs):
     groups, times = beams_ref.shape[0], beams_ref.shape[1]
-    stations, samples = beams_ref.shape[3], beams_ref.shape[4]
-    row_groups = out_ref.shape[1] // stations
+    row_count = out_refs[0].shape[0]
+    row_groups = row_count // beams_ref.shape[3]
     first = row_ref[0] * row_groups
+    order = [lax.rem(first + (g ^ 1), groups) for g in range(groups)]
     total = None
     for t in range(times):
-        re = jnp.concatenate([beams_ref[g ^ 1, t, 0] for g in range(groups)], axis=0)
-        im = jnp.concatenate([beams_ref[g ^ 1, t, 1] for g in range(groups)], axis=0)
-        left = jnp.concatenate([re, im], axis=-1)
-        row_re = jnp.concatenate([beams_ref[first + (g ^ 1), t, 0] for g in range(row_groups)], axis=0)
-        row_im = jnp.concatenate([beams_ref[first + (g ^ 1), t, 1] for g in range(row_groups)], axis=0)
+        re = [beams_ref[g, t, 0] for g in order]
+        im = [beams_ref[g, t, 1] for g in order]
+        left = jnp.concatenate([jnp.concatenate(re, axis=0), jnp.concatenate(im, axis=0)], axis=-1)
+        row_re = jnp.concatenate(re[:row_groups], axis=0)
+        row_im = jnp.concatenate(im[:row_groups], axis=0)
         left_rows = jnp.concatenate([row_re, row_im], axis=-1)
         other_rows = jnp.concatenate([row_im, -row_re], axis=-1)
         rows = jnp.concatenate([left_rows, other_rows], axis=0)
         part = lax.dot_general(rows, left, NT_DIMS, preferred_element_type=jnp.float32)
         total = part if total is None else total + part
-    out_ref[...] = (total * scale).reshape(out_ref.shape).astype(out_ref.dtype)
+    total = total * scale
+    re, im = total[:row_count], total[row_count:]
+    if packed:
+        upper, _ = triangles(row_count)
+        diagonal = jnp.where(upper, re[:, :row_count], im[:, :row_count])
+        out_refs[0][:, :row_count] = diagonal.astype(out_refs[0].dtype)
+        out_refs[0][:, row_count:] = re[:, row_count:].astype(out_refs[0].dtype)
+        out_refs[1][...] = im[:, row_count:].astype(out_refs[1].dtype)
+    else:
+        out_refs[0][...] = re.astype(out_refs[0].dtype)
+        out_refs[1][...] = im.astype(out_refs[1].dtype)
 
 
-def correlate_rows(row, beams, rows, columns, scale, dtype, name):
+def triangles(size):
+    i = lax.broadcasted_iota(jnp.int32, (size, size), 0)
+    j = lax.broadcasted_iota(jnp.int32, (size, size), 1)
+    return i <= j, i > j
+
+
+def correlate_rows(row, beams, rows, columns, scale, packed, dtype, name):
+    second = columns - rows if packed else columns
     return pl.pallas_call(
-        lambda *refs: correlate(scale, *refs),
-        out_shape=jax.ShapeDtypeStruct((2, rows, columns), dtype),
+        lambda *refs: correlate(scale, packed, *refs),
+        out_shape=[jax.ShapeDtypeStruct((rows, columns), dtype), jax.ShapeDtypeStruct((rows, second), dtype)],
         in_specs=[pl.BlockSpec(memory_space=pltpu.SMEM), pl.BlockSpec(memory_space=pltpu.VMEM)],
-        out_specs=pl.BlockSpec(memory_space=pltpu.VMEM),
+        out_specs=[pl.BlockSpec(memory_space=pltpu.VMEM)] * 2,
         compiler_params=pltpu.CompilerParams(vmem_limit_bytes=16 * 2**20),
         cost_estimate=pl.CostEstimate(flops=4 * rows * columns * 512, bytes_accessed=2**20, transcendentals=0),
         name=name,
     )(row, beams)
+
+
+def add_rows(part, row_ref, ours_ref, *refs):
+    out_hbm, total, sems = refs[-3:]
+    rows, columns = total.shape
+    blocks = columns // rows
+    both = refs[0][:, :rows].astype(jnp.float32)
+    mirrored = both.T
+    upper, lower = triangles(rows)
+    stores = []
+    for k in list(range(1, blocks)) + [0]:
+        at = pl.ds(k * rows, rows)
+        if k == 0:
+            if part == 0:
+                block = jnp.where(upper, both, mirrored)
+            else:
+                block = jnp.where(lower, both, 0.0) - jnp.where(lower, both, 0.0).T
+        elif part == 0:
+            block = refs[0][:, at].astype(jnp.float32)
+        else:
+            block = refs[1][:, pl.ds((k - 1) * rows, rows)].astype(jnp.float32)
+        total[:, at] = ours_ref[:, at] + block
+        place = pl.multiple_of(lax.rem(row_ref[0] + k, blocks) * rows, rows)
+        stores.append(pltpu.make_async_copy(total.at[:, at], out_hbm.at[part, :, pl.ds(place, rows)], sems.at[k]))
+        stores[-1].start()
+    for store in stores:
+        store.wait()
+
+
+def add_part(part, row, ours, arrived, result):
+    rows, columns = ours.shape
+    vmem = pl.BlockSpec(memory_space=pltpu.VMEM)
+    hbm = pl.BlockSpec(memory_space=pltpu.HBM)
+    return pl.pallas_call(
+        lambda *refs: add_rows(part, *refs),
+        out_shape=jax.ShapeDtypeStruct((2, rows, columns), jnp.float32),
+        in_specs=[pl.BlockSpec(memory_space=pltpu.SMEM), vmem] + [vmem] * len(arrived) + [hbm] * len(result),
+        out_specs=hbm,
+        scratch_shapes=[pltpu.VMEM((rows, columns), jnp.float32), pltpu.SemaphoreType.DMA((columns // rows,))],
+        input_output_aliases={2 + len(arrived): 0} if result else {},
+        compiler_params=pltpu.CompilerParams(vmem_limit_bytes=16 * 2**20),
+        cost_estimate=pl.CostEstimate(flops=rows * columns, bytes_accessed=8 * rows * columns, transcendentals=0),
+        name="add_re" if part == 0 else "add_im",
+    )(row, ours, *arrived, *result)
 
 
 def local(voltages, weights):
@@ -104,10 +166,13 @@
     columns = groups * stations
     rows = columns // times
     scale = 1.0 / (samples * times)
-    theirs = correlate_rows(row ^ 1, turned, rows, columns, scale, jnp.bfloat16, "correlate_theirs")
-    arrived = lax.ppermute(theirs, "tchunk", [(t, t ^ 1) for t in range(times)])
-    ours = correlate_rows(row, turned, rows, columns, scale, jnp.float32, "correlate_ours")
-    return (ours + arrived.astype(jnp.float32))[:, None, None]
+    theirs = correlate_rows(row ^ 1, turned, rows, columns, scale, True, jnp.bfloat16, "correlate_theirs")
+    swap = [(t, t ^ 1) for t in range(times)]
+    arrived = [lax.ppermute(part, "tchunk", swap) for part in theirs]
+    ours = correlate_rows(row, turned, rows, columns, scale, False, jnp.float32, "correlate_ours")
+    result = add_part(0, row, ours[0], arrived[:1], [])
+    result = add_part(1, row, ours[1], arrived, [result])
+    return result[:, None, None]
 
 
 def solution(mesh):

time: 49.9 us -> 49.3 us (0.988)
  waiting for transfers between devices: 26.3 us -> 21.9 us
  starting transfers between devices: 18.4 us -> 21.7 us
  Pallas kernels: 3.79 us -> 5.36 us
  other arithmetic: 0.87 us -> 0 us
    ppermute x1 -> x2, waiting for transfers between devices: 6.49 us -> 2.13 us  [local(): arrived = [lax.ppermute(part, 'tchunk', swap) for part in theirs]]
    ppermute x1 -> x2, starting transfers between devices: 1.92 us -> 5.28 us  [local(): arrived = [lax.ppermute(part, 'tchunk', swap) for part in theirs]]
    pallas_call x2 -> x4, Pallas kernels: 0.66 us -> 2.23 us  [the longest x2 1.55 us: add_part(): pl.pallas_call(lambda *refs: add_rows(part, *refs), out_shape=jax.ShapeDt...]
    broadcast_in_dim x1 -> x0, other arithmetic: 0.87 us -> none  [local(): return (ours + arrived.astype(jnp.float32))[:, None, None]]
  transfers between devices with their start and end apart: 2 -> 3, of which waited for: 2 -> 3; matrix products, arithmetic and copies ran while one was open for 0% -> 0% of each run, Pallas kernels for 1% -> 2%
where the time goes in v4:
time: 49.3 us; the launch traced here: 49.1 us
  waiting for transfers between devices  21.9 us (44%)
  starting transfers between devices  21.7 us (44%)
  Pallas kernels  5.36 us (11%)
    all_to_all x1, waiting for transfers between devices, local(): lax.all_to_all(formed, ('stn', 'tchunk'), 0, 0, axis_index_groups=classes...  19.8 us
    all_to_all x1, starting transfers between devices, local(): lax.all_to_all(formed, ('stn', 'tchunk'), 0, 0, axis_index_groups=classes...  16.5 us
    ppermute x2, starting transfers between devices, local(): arrived = [lax.ppermute(part, 'tchunk', swap) for part in theirs]  5.28 us
    pallas_call x1, Pallas kernels, local(): pl.pallas_call(lambda *refs: form_beams(times // 2, pieces, *refs), out_s...  3.13 us
    ppermute x2, waiting for transfers between devices, local(): arrived = [lax.ppermute(part, 'tchunk', swap) for part in theirs]  2.13 us
    pallas_call x2, Pallas kernels, add_part(): pl.pallas_call(lambda *refs: add_rows(part, *refs), out_shape=jax.ShapeDt...  1.55 us
  transfers between devices with their start and end apart: 3, of which 3 were waited for; matrix products, arithmetic and copies ran while one was open for 0% of the time, Pallas kernels for 2%

profile of v4, /device:TPU:1, one launch (start us, length us, event | category | flops | bytes accessed | tf_op | source)
XLA Modules:
  0.0 49.1 jit_solution(12551532491261920303)
XLA Ops:
  0.0 3.1 %form_beams.1 = bf16[32,2,2,16,128]{4,3,2,1,0:T(8,128)(2,1)} custom-call(bf16[16,128,512]{2,1,0:T(8,128)(2,1)} %bitcast.10, bf16[16,2,32,256]{3,2,1,0:T(8,128)(2,1)} %bitcast.11), custom_call_target="tpu_custom_call" | custom-call | tf_op jit(solution)/shard_map/form_beams/pallas_call | solution.py:144
  3.1 16.5 %all-to-all-start = ((bf16[64,2,16,128]{3,2,1,0:T(8,128)(2,1)}), bf16[64,2,16,128]{3,2,1,0:T(8,128)(2,1)S(1)}, u32[]{:S(2)}, u32[]{:S(2)}) async-start(bf16[64,2,16,128]{3,2,1,0:T(8,128)(2,1)} %bitcast.3), calls=%async_computation | async-start | bytes 1048576 | tf_op jit(solution)/shard_map/all_to_all | solution.py:163
  19.6 19.8 %all-to-all-done = bf16[64,2,16,128]{3,2,1,0:T(8,128)(2,1)S(1)} async-done(((bf16[64,2,16,128]{3,2,1,0:T(8,128)(2,1)}), bf16[64,2,16,128]{3,2,1,0:T(8,128)(2,1)S(1)}, u32[]{:S(2)}, u32[]{:S(2)}) %all-to-all-start) | async-done | bytes 524320 | tf_op jit(solution)/shard_map/all_to_all | solution.py:163
  39.4 0.3 correlate_theirs.1
  39.7 1.9 %collective-permute-start = (bf16[128,512]{1,0:T(8,128)(2,1)S(1)}, bf16[128,512]{1,0:T(8,128)(2,1)S(1)}, u32[]{:S(2)}, u32[]{:S(2)}) collective-permute-start(bf16[128,512]{1,0:T(8,128)(2,1)S(1)} %get-tuple-element.10), channel_id=1, source_target_pairs={{0,1},{1,0},{2,3},{3,2},{4,5},{5,4},{6,7},{7,6},{8,9},{9,8},{10,11... | collective-permute-start | bytes 393224 | tf_op jit(solution)/shard_map/ppermute | solution.py:171
  41.6 3.4 %collective-permute-start.1 = (bf16[128,384]{1,0:T(8,128)(2,1)S(1)}, bf16[128,384]{1,0:T(8,128)(2,1)S(1)}, u32[]{:S(2)}, u32[]{:S(2)}) collective-permute-start(bf16[128,384]{1,0:T(8,128)(2,1)S(1)} %get-tuple-element.11), channel_id=1, source_target_pairs={{0,1},{1,0},{2,3},{3,2},{4,5},{5,4},{6,7},{7,6},{8,9},{9,8},{10,11... | collective-permute-start | bytes 294920 | tf_op jit(solution)/shard_map/ppermute | solution.py:171
  45.0 0.4 correlate_ours.1
  45.4 0.1 collective-permute-done.refs_2_
  45.4 0.8 %add_re.1.refs_4_ = f32[2,128,512]{2,1,0:T(8,128)} custom-call(s32[1]{0:T(128)} %bitcast.refs_0_, f32[128,512]{1,0:T(8,128)S(1)} %get-tuple-element.12.refs_1_, bf16[128,512]{1,0:T(8,128)(2,1)S(1)} %collective-permute-done.refs_2_), custom_call_target="tpu_custom_call" | custom-call | flops 65536 | bytes 524288 | tf_op jit(solution)/shard_map/add_re/pallas_call | solution.py:124
  46.2 2.1 %collective-permute-done.1.refs_3_ = bf16[128,384]{1,0:T(8,128)(2,1)S(1)} collective-permute-done((bf16[128,384]{1,0:T(8,128)(2,1)S(1)}, bf16[128,384]{1,0:T(8,128)(2,1)S(1)}, u32[]{:S(2)}, u32[]{:S(2)}) %collective-permute-start.1) | collective-permute-done | bytes 98336 | tf_op jit(solution)/shard_map/ppermute | solution.py:171
  48.3 0.8 %add_im.1 = f32[2,128,512]{2,1,0:T(8,128)} custom-call(s32[1]{0:T(128)} %bitcast.refs_0_, f32[128,512]{1,0:T(8,128)S(1)} %get-tuple-element.9.refs_1_, bf16[128,512]{1,0:T(8,128)(2,1)S(1)} %collective-permute-done.refs_2_, bf16[128,384]{1,0:T(8,128)(2,1)S(1)} %collective-permute-done.1.refs_3_, ...), custom_call_target="tpu_custom_call", output_to_operand_aliasing={{}: (4, {})} | custom-call | flops 65536 | bytes 524288 | tf_op jit(solution)/shard_map/add_im/pallas_call | solution.py:124
Async XLA Ops:
  3.1 36.2 %all-to-all-start = ((bf16[64,2,16,128]{3,2,1,0:T(8,128)(2,1)}), bf16[64,2,16,128]{3,2,1,0:T(8,128)(2,1)S(1)}, u32[]{:S(2)}, u32[]{:S(2)}) async-start(bf16[64,2,16,128]{3,2,1,0:T(8,128)(2,1)} %bitcast.3), calls=%async_computation | async-start | bytes 1048576 | tf_op jit(solution)/shard_map/all_to_all | solution.py:163
  39.7 5.7 %collective-permute-start = (bf16[128,512]{1,0:T(8,128)(2,1)S(1)}, bf16[128,512]{1,0:T(8,128)(2,1)S(1)}, u32[]{:S(2)}, u32[]{:S(2)}) collective-permute-start(bf16[128,512]{1,0:T(8,128)(2,1)S(1)} %get-tuple-element.10), channel_id=1, source_target_pairs={{0,1},{1,0},{2,3},{3,2},{4,5},{5,4},{6,7},{7,6},{8,9},{9,8},{10,11... | collective-permute-start | bytes 393224 | tf_op jit(solution)/shard_map/ppermute | solution.py:171
  41.6 6.6 %collective-permute-start.1 = (bf16[128,384]{1,0:T(8,128)(2,1)S(1)}, bf16[128,384]{1,0:T(8,128)(2,1)S(1)}, u32[]{:S(2)}, u32[]{:S(2)}) collective-permute-start(bf16[128,384]{1,0:T(8,128)(2,1)S(1)} %get-tuple-element.11), channel_id=1, source_target_pairs={{0,1},{1,0},{2,3},{3,2},{4,5},{5,4},{6,7},{7,6},{8,9},{9,8},{10,11... | collective-permute-start | bytes 294920 | tf_op jit(solution)/shard_map/ppermute | solution.py:171

commit v5 on v4

--- a/solution.py
+++ b/solution.py
@@ -6,6 +6,7 @@
 from jax.sharding import PartitionSpec as P
 
 NT_DIMS = (((1,), (1,)), ((), ()))
+LAST = 2
 
 
 def form_beams(copies, pieces, volt_hbm, wgt_hbm, out_ref, volt_ref, wgt_ref, held, sems):
@@ -42,7 +43,7 @@
 
 def correlate(scale, packed, row_ref, beams_ref, *out_refs):
     groups, times = beams_ref.shape[0], beams_ref.shape[1]
-    row_count = out_refs[0].shape[0]
+    row_count, columns = out_refs[0].shape[0], groups * beams_ref.shape[3]
     row_groups = row_count // beams_ref.shape[3]
     first = row_ref[0] * row_groups
     order = [lax.rem(first + (g ^ 1), groups) for g in range(groups)]
@@ -63,12 +64,20 @@
     if packed:
         upper, _ = triangles(row_count)
         diagonal = jnp.where(upper, re[:, :row_count], im[:, :row_count])
-        out_refs[0][:, :row_count] = diagonal.astype(out_refs[0].dtype)
-        out_refs[0][:, row_count:] = re[:, row_count:].astype(out_refs[0].dtype)
-        out_refs[1][...] = im[:, row_count:].astype(out_refs[1].dtype)
+        for (part, k), (to, at) in places(columns // row_count, row_count).items():
+            block = (re, im)[part][:, k * row_count : (k + 1) * row_count]
+            if k == 0:
+                block = diagonal
+            out_refs[to][:, at] = block.astype(out_refs[to].dtype)
     else:
         out_refs[0][...] = re.astype(out_refs[0].dtype)
         out_refs[1][...] = im.astype(out_refs[1].dtype)
+
+
+def places(blocks, size):
+    order = [(0, k) for k in range(blocks)] + [(1, k) for k in range(1, blocks)]
+    first = len(order) - LAST
+    return {b: (int(n >= first), slice((n % first) * size, (n % first + 1) * size)) for n, b in enumerate(order)}
 
 
 def triangles(size):
@@ -78,10 +87,10 @@
 
 
 def correlate_rows(row, beams, rows, columns, scale, packed, dtype, name):
-    second = columns - rows if packed else columns
+    widths = (2 * columns - (1 + LAST) * rows, LAST * rows) if packed else (columns, columns)
     return pl.pallas_call(
         lambda *refs: correlate(scale, packed, *refs),
-        out_shape=[jax.ShapeDtypeStruct((rows, columns), dtype), jax.ShapeDtypeStruct((rows, second), dtype)],
+        out_shape=[jax.ShapeDtypeStruct((rows, width), dtype) for width in widths],
         in_specs=[pl.BlockSpec(memory_space=pltpu.SMEM), pl.BlockSpec(memory_space=pltpu.VMEM)],
         out_specs=[pl.BlockSpec(memory_space=pltpu.VMEM)] * 2,
         compiler_params=pltpu.CompilerParams(vmem_limit_bytes=16 * 2**20),
@@ -90,48 +99,44 @@
     )(row, beams)
 
 
-def add_rows(part, row_ref, ours_ref, *refs):
+def add_rows(stage, row_ref, re_ref, im_ref, arrived_ref, *refs):
     out_hbm, total, sems = refs[-3:]
-    rows, columns = total.shape
+    rows, columns = re_ref.shape
     blocks = columns // rows
-    both = refs[0][:, :rows].astype(jnp.float32)
-    mirrored = both.T
-    upper, lower = triangles(rows)
+    here = [(b, at) for b, (to, at) in places(blocks, rows).items() if to == stage and b[1] > 0]
+    if stage == 0:
+        both = arrived_ref[:, :rows].astype(jnp.float32)
+        upper, lower = triangles(rows)
+        strict = jnp.where(lower, both, 0.0)
+        here += [((0, 0), jnp.where(upper, both, both.T)), ((1, 0), strict - strict.T)]
     stores = []
-    for k in list(range(1, blocks)) + [0]:
-        at = pl.ds(k * rows, rows)
-        if k == 0:
-            if part == 0:
-                block = jnp.where(upper, both, mirrored)
-            else:
-                block = jnp.where(lower, both, 0.0) - jnp.where(lower, both, 0.0).T
-        elif part == 0:
-            block = refs[0][:, at].astype(jnp.float32)
-        else:
-            block = refs[1][:, pl.ds((k - 1) * rows, rows)].astype(jnp.float32)
-        total[:, at] = ours_ref[:, at] + block
+    for n, ((part, k), block) in enumerate(here):
+        if k > 0:
+            block = arrived_ref[:, block].astype(jnp.float32)
+        total[n] = (re_ref, im_ref)[part][:, k * rows : (k + 1) * rows] + block
         place = pl.multiple_of(lax.rem(row_ref[0] + k, blocks) * rows, rows)
-        stores.append(pltpu.make_async_copy(total.at[:, at], out_hbm.at[part, :, pl.ds(place, rows)], sems.at[k]))
+        stores.append(pltpu.make_async_copy(total.at[n], out_hbm.at[part, :, pl.ds(place, rows)], sems.at[n]))
         stores[-1].start()
     for store in stores:
         store.wait()
 
 
-def add_part(part, row, ours, arrived, result):
-    rows, columns = ours.shape
+def add_part(stage, row, ours, arrived, result):
+    rows, columns = ours[0].shape
     vmem = pl.BlockSpec(memory_space=pltpu.VMEM)
     hbm = pl.BlockSpec(memory_space=pltpu.HBM)
+    count = LAST if stage else 2 * (columns // rows) - LAST
     return pl.pallas_call(
-        lambda *refs: add_rows(part, *refs),
+        lambda *refs: add_rows(stage, *refs),
         out_shape=jax.ShapeDtypeStruct((2, rows, columns), jnp.float32),
-        in_specs=[pl.BlockSpec(memory_space=pltpu.SMEM), vmem] + [vmem] * len(arrived) + [hbm] * len(result),
+        in_specs=[pl.BlockSpec(memory_space=pltpu.SMEM), vmem, vmem, vmem] + [hbm] * len(result),
         out_specs=hbm,
-        scratch_shapes=[pltpu.VMEM((rows, columns), jnp.float32), pltpu.SemaphoreType.DMA((columns // rows,))],
-        input_output_aliases={2 + len(arrived): 0} if result else {},
+        scratch_shapes=[pltpu.VMEM((count, rows, rows), jnp.float32), pltpu.SemaphoreType.DMA((count,))],
+        input_output_aliases={4: 0} if result else {},
         compiler_params=pltpu.CompilerParams(vmem_limit_bytes=16 * 2**20),
         cost_estimate=pl.CostEstimate(flops=rows * columns, bytes_accessed=8 * rows * columns, transcendentals=0),
-        name="add_re" if part == 0 else "add_im",
-    )(row, ours, *arrived, *result)
+        name="add_last" if stage else "add_first",
+    )(row, *ours, arrived, *result)
 
 
 def local(voltages, weights):
@@ -170,8 +175,8 @@
     swap = [(t, t ^ 1) for t in range(times)]
     arrived = [lax.ppermute(part, "tchunk", swap) for part in theirs]
     ours = correlate_rows(row, turned, rows, columns, scale, False, jnp.float32, "correlate_ours")
-    result = add_part(0, row, ours[0], arrived[:1], [])
-    result = add_part(1, row, ours[1], arrived, [result])
+    result = add_part(0, row, ours, arrived[0], [])
+    result = add_part(1, row, ours, arrived[1], [result])
     return result[:, None, None]
 
 

time: 49.3 us -> 49 us (level)
  waiting for transfers between devices: 21.9 us -> 21.3 us
    ppermute x2, waiting for transfers between devices: 2.13 us -> 1.58 us  [local(): arrived = [lax.ppermute(part, 'tchunk', swap) for part in theirs]]
where the time goes in v5:
time: 49 us; the launch traced here: 48.4 us
  starting transfers between devices  21.7 us (44%)
  waiting for transfers between devices  21.3 us (43%)
  Pallas kernels  5.31 us (11%)
    all_to_all x1, waiting for transfers between devices, local(): lax.all_to_all(formed, ('stn', 'tchunk'), 0, 0, axis_index_groups=classes...  19.8 us
    all_to_all x1, starting transfers between devices, local(): lax.all_to_all(formed, ('stn', 'tchunk'), 0, 0, axis_index_groups=classes...  16.5 us
    ppermute x2, starting transfers between devices, local(): arrived = [lax.ppermute(part, 'tchunk', swap) for part in theirs]  5.28 us
    pallas_call x1, Pallas kernels, local(): pl.pallas_call(lambda *refs: form_beams(times // 2, pieces, *refs), out_s...  3.13 us
    ppermute x2, waiting for transfers between devices, local(): arrived = [lax.ppermute(part, 'tchunk', swap) for part in theirs]  1.58 us
    pallas_call x2, Pallas kernels, add_part(): pl.pallas_call(lambda *refs: add_rows(stage, *refs), out_shape=jax.ShapeD...  1.5 us
  transfers between devices with their start and end apart: 3, of which 3 were waited for; matrix products, arithmetic and copies ran while one was open for 0% of the time, Pallas kernels for 2%

profile of v5, /device:TPU:1, one launch (start us, length us, event | category | flops | bytes accessed | tf_op | source)
XLA Modules:
  0.0 48.4 jit_solution(11881293371302183520)
XLA Ops:
  0.0 3.1 %form_beams.1 = bf16[32,2,2,16,128]{4,3,2,1,0:T(8,128)(2,1)} custom-call(bf16[16,128,512]{2,1,0:T(8,128)(2,1)} %bitcast.10, bf16[16,2,32,256]{3,2,1,0:T(8,128)(2,1)} %bitcast.11), custom_call_target="tpu_custom_call" | custom-call | tf_op jit(solution)/shard_map/form_beams/pallas_call | solution.py:149
  3.1 16.5 %all-to-all-start = ((bf16[64,2,16,128]{3,2,1,0:T(8,128)(2,1)}), bf16[64,2,16,128]{3,2,1,0:T(8,128)(2,1)S(1)}, u32[]{:S(2)}, u32[]{:S(2)}) async-start(bf16[64,2,16,128]{3,2,1,0:T(8,128)(2,1)} %bitcast.3), calls=%async_computation | async-start | bytes 1048576 | tf_op jit(solution)/shard_map/all_to_all | solution.py:168
  19.6 19.8 %all-to-all-done = bf16[64,2,16,128]{3,2,1,0:T(8,128)(2,1)S(1)} async-done(((bf16[64,2,16,128]{3,2,1,0:T(8,128)(2,1)}), bf16[64,2,16,128]{3,2,1,0:T(8,128)(2,1)S(1)}, u32[]{:S(2)}, u32[]{:S(2)}) %all-to-all-start) | async-done | bytes 524320 | tf_op jit(solution)/shard_map/all_to_all | solution.py:168
  39.4 0.3 correlate_theirs.1
  39.7 1.9 %collective-permute-start.1 = (bf16[128,640]{1,0:T(8,128)(2,1)S(1)}, bf16[128,640]{1,0:T(8,128)(2,1)S(1)}, u32[]{:S(2)}, u32[]{:S(2)}) collective-permute-start(bf16[128,640]{1,0:T(8,128)(2,1)S(1)} %get-tuple-element.12), channel_id=1, source_target_pairs={{0,1},{1,0},{2,3},{3,2},{4,5},{5,4},{6,7},{7,6},{8,9},{9,8},{10,11... | collective-permute-start | bytes 491528 | tf_op jit(solution)/shard_map/ppermute | solution.py:176
  41.6 3.4 %collective-permute-start = (bf16[128,256]{1,0:T(8,128)(2,1)S(1)}, bf16[128,256]{1,0:T(8,128)(2,1)S(1)}, u32[]{:S(2)}, u32[]{:S(2)}) collective-permute-start(bf16[128,256]{1,0:T(8,128)(2,1)S(1)} %get-tuple-element.11), channel_id=1, source_target_pairs={{0,1},{1,0},{2,3},{3,2},{4,5},{5,4},{6,7},{7,6},{8,9},{9,8},{10,11... | collective-permute-start | bytes 196616 | tf_op jit(solution)/shard_map/ppermute | solution.py:176
  45.0 0.4 correlate_ours.1
  45.4 1.0 %collective-permute-done.1.refs_3_ = bf16[128,640]{1,0:T(8,128)(2,1)S(1)} collective-permute-done((bf16[128,640]{1,0:T(8,128)(2,1)S(1)}, bf16[128,640]{1,0:T(8,128)(2,1)S(1)}, u32[]{:S(2)}, u32[]{:S(2)}) %collective-permute-start.1) | collective-permute-done | bytes 163872 | tf_op jit(solution)/shard_map/ppermute | solution.py:176
  46.4 0.8 %add_first.1.refs_4_ = f32[2,128,512]{2,1,0:T(8,128)} custom-call(s32[1]{0:T(128)} %bitcast.refs_0_, f32[128,512]{1,0:T(8,128)S(1)} %get-tuple-element.9.refs_1_, f32[128,512]{1,0:T(8,128)S(1)} %get-tuple-element.10.refs_2_, bf16[128,640]{1,0:T(8,128)(2,1)S(1)} %collective-permute-done.1.refs_3_), custom_call_target="tpu_custom_call" | custom-call | flops 65536 | bytes 524288 | tf_op jit(solution)/shard_map/add_first/pallas_call | solution.py:129
  47.2 0.6 %collective-permute-done.refs_3_ = bf16[128,256]{1,0:T(8,128)(2,1)S(1)} collective-permute-done((bf16[128,256]{1,0:T(8,128)(2,1)S(1)}, bf16[128,256]{1,0:T(8,128)(2,1)S(1)}, u32[]{:S(2)}, u32[]{:S(2)}) %collective-permute-start) | collective-permute-done | bytes 65568 | tf_op jit(solution)/shard_map/ppermute | solution.py:176
  47.8 0.7 %add_last.1 = f32[2,128,512]{2,1,0:T(8,128)} custom-call(s32[1]{0:T(128)} %bitcast.refs_0_, f32[128,512]{1,0:T(8,128)S(1)} %get-tuple-element.9.refs_1_, f32[128,512]{1,0:T(8,128)S(1)} %get-tuple-element.10.refs_2_, bf16[128,256]{1,0:T(8,128)(2,1)S(1)} %collective-permute-done.refs_3_, f32[2,128,512]{2,1,0:T(8,128)} %add_first.1.refs_4_), custom_call_target="tpu_custom_call", output_to_operand_aliasing={{}: (4, {})} | custom-call | flops 65536 | bytes 524288 | tf_op jit(solution)/shard_map/add_last/pallas_call | solution.py:129
Async XLA Ops:
  3.1 36.2 %all-to-all-start = ((bf16[64,2,16,128]{3,2,1,0:T(8,128)(2,1)}), bf16[64,2,16,128]{3,2,1,0:T(8,128)(2,1)S(1)}, u32[]{:S(2)}, u32[]{:S(2)}) async-start(bf16[64,2,16,128]{3,2,1,0:T(8,128)(2,1)} %bitcast.3), calls=%async_computation | async-start | bytes 1048576 | tf_op jit(solution)/shard_map/all_to_all | solution.py:168
  39.7 6.7 %collective-permute-start.1 = (bf16[128,640]{1,0:T(8,128)(2,1)S(1)}, bf16[128,640]{1,0:T(8,128)(2,1)S(1)}, u32[]{:S(2)}, u32[]{:S(2)}) collective-permute-start(bf16[128,640]{1,0:T(8,128)(2,1)S(1)} %get-tuple-element.12), channel_id=1, source_target_pairs={{0,1},{1,0},{2,3},{3,2},{4,5},{5,4},{6,7},{7,6},{8,9},{9,8},{10,11... | collective-permute-start | bytes 491528 | tf_op jit(solution)/shard_map/ppermute | solution.py:176
  41.6 6.1 %collective-permute-start = (bf16[128,256]{1,0:T(8,128)(2,1)S(1)}, bf16[128,256]{1,0:T(8,128)(2,1)S(1)}, u32[]{:S(2)}, u32[]{:S(2)}) collective-permute-start(bf16[128,256]{1,0:T(8,128)(2,1)S(1)} %get-tuple-element.11), channel_id=1, source_target_pairs={{0,1},{1,0},{2,3},{3,2},{4,5},{5,4},{6,7},{7,6},{8,9},{9,8},{10,11... | collective-permute-start | bytes 196616 | tf_op jit(solution)/shard_map/ppermute | solution.py:176

commit v6 on v5

--- a/solution.py
+++ b/solution.py
@@ -6,7 +6,6 @@
 from jax.sharding import PartitionSpec as P
 
 NT_DIMS = (((1,), (1,)), ((), ()))
-LAST = 2
 
 
 def form_beams(copies, pieces, volt_hbm, wgt_hbm, out_ref, volt_ref, wgt_ref, held, sems):
@@ -64,11 +63,11 @@
     if packed:
         upper, _ = triangles(row_count)
         diagonal = jnp.where(upper, re[:, :row_count], im[:, :row_count])
-        for (part, k), (to, at) in places(columns // row_count, row_count).items():
+        for (part, k), at in places(columns // row_count, row_count).items():
             block = (re, im)[part][:, k * row_count : (k + 1) * row_count]
             if k == 0:
                 block = diagonal
-            out_refs[to][:, at] = block.astype(out_refs[to].dtype)
+            out_refs[0][:, at] = block.astype(out_refs[0].dtype)
     else:
         out_refs[0][...] = re.astype(out_refs[0].dtype)
         out_refs[1][...] = im.astype(out_refs[1].dtype)
@@ -76,8 +75,7 @@
 
 def places(blocks, size):
     order = [(0, k) for k in range(blocks)] + [(1, k) for k in range(1, blocks)]
-    first = len(order) - LAST
-    return {b: (int(n >= first), slice((n % first) * size, (n % first + 1) * size)) for n, b in enumerate(order)}
+    return {b: slice(n * size, (n + 1) * size) for n, b in enumerate(order)}
 
 
 def triangles(size):
@@ -87,32 +85,32 @@
 
 
 def correlate_rows(row, beams, rows, columns, scale, packed, dtype, name):
-    widths = (2 * columns - (1 + LAST) * rows, LAST * rows) if packed else (columns, columns)
+    widths = (2 * columns - rows,) if packed else (columns, columns)
     return pl.pallas_call(
         lambda *refs: correlate(scale, packed, *refs),
         out_shape=[jax.ShapeDtypeStruct((rows, width), dtype) for width in widths],
         in_specs=[pl.BlockSpec(memory_space=pltpu.SMEM), pl.BlockSpec(memory_space=pltpu.VMEM)],
-        out_specs=[pl.BlockSpec(memory_space=pltpu.VMEM)] * 2,
+        out_specs=[pl.BlockSpec(memory_space=pltpu.VMEM)] * len(widths),
         compiler_params=pltpu.CompilerParams(vmem_limit_bytes=16 * 2**20),
         cost_estimate=pl.CostEstimate(flops=4 * rows * columns * 512, bytes_accessed=2**20, transcendentals=0),
         name=name,
     )(row, beams)
 
 
-def add_rows(stage, row_ref, re_ref, im_ref, arrived_ref, *refs):
+def add_rows(row_ref, re_ref, im_ref, *refs):
     out_hbm, total, sems = refs[-3:]
+    arrived_refs = refs[:-3]
     rows, columns = re_ref.shape
     blocks = columns // rows
-    here = [(b, at) for b, (to, at) in places(blocks, rows).items() if to == stage and b[1] > 0]
-    if stage == 0:
-        both = arrived_ref[:, :rows].astype(jnp.float32)
-        upper, lower = triangles(rows)
-        strict = jnp.where(lower, both, 0.0)
-        here += [((0, 0), jnp.where(upper, both, both.T)), ((1, 0), strict - strict.T)]
+    both = arrived_refs[0][:, :rows].astype(jnp.float32)
+    upper, lower = triangles(rows)
+    strict = jnp.where(lower, both, 0.0)
+    here = [(b, at) for b, at in places(blocks, rows).items() if b[1] > 0]
+    here += [((0, 0), jnp.where(upper, both, both.T)), ((1, 0), strict - strict.T)]
     stores = []
     for n, ((part, k), block) in enumerate(here):
         if k > 0:
-            block = arrived_ref[:, block].astype(jnp.float32)
+            block = arrived_refs[0][:, block].astype(jnp.float32)
         total[n] = (re_ref, im_ref)[part][:, k * rows : (k + 1) * rows] + block
         place = pl.multiple_of(lax.rem(row_ref[0] + k, blocks) * rows, rows)
         stores.append(pltpu.make_async_copy(total.at[n], out_hbm.at[part, :, pl.ds(place, rows)], sems.at[n]))
@@ -121,22 +119,20 @@
         store.wait()
 
 
-def add_part(stage, row, ours, arrived, result):
+def add_parts(row, ours, arrived):
     rows, columns = ours[0].shape
     vmem = pl.BlockSpec(memory_space=pltpu.VMEM)
-    hbm = pl.BlockSpec(memory_space=pltpu.HBM)
-    count = LAST if stage else 2 * (columns // rows) - LAST
+    count = 2 * (columns // rows)
     return pl.pallas_call(
-        lambda *refs: add_rows(stage, *refs),
+        add_rows,
         out_shape=jax.ShapeDtypeStruct((2, rows, columns), jnp.float32),
-        in_specs=[pl.BlockSpec(memory_space=pltpu.SMEM), vmem, vmem, vmem] + [hbm] * len(result),
-        out_specs=hbm,
+        in_specs=[pl.BlockSpec(memory_space=pltpu.SMEM)] + [vmem] * (2 + len(arrived)),
+        out_specs=pl.BlockSpec(memory_space=pltpu.HBM),
         scratch_shapes=[pltpu.VMEM((count, rows, rows), jnp.float32), pltpu.SemaphoreType.DMA((count,))],
-        input_output_aliases={4: 0} if result else {},
         compiler_params=pltpu.CompilerParams(vmem_limit_bytes=16 * 2**20),
         cost_estimate=pl.CostEstimate(flops=rows * columns, bytes_accessed=8 * rows * columns, transcendentals=0),
-        name="add_last" if stage else "add_first",
-    )(row, *ours, arrived, *result)
+        name="add_parts",
+    )(row, *ours, *arrived)
 
 
 def local(voltages, weights):
@@ -175,8 +171,7 @@
     swap = [(t, t ^ 1) for t in range(times)]
     arrived = [lax.ppermute(part, "tchunk", swap) for part in theirs]
     ours = correlate_rows(row, turned, rows, columns, scale, False, jnp.float32, "correlate_ours")
-    result = add_part(0, row, ours, arrived[0], [])
-    result = add_part(1, row, ours, arrived[1], [result])
+    result = add_parts(row, ours, arrived)
     return result[:, None, None]
 
 

time: 49 us -> 49.2 us (level)
  waiting for transfers between devices: 21.3 us -> 25.5 us
  starting transfers between devices: 21.7 us -> 18.4 us
  Pallas kernels: 5.31 us -> 4.69 us
    ppermute x2 -> x1, waiting for transfers between devices: 1.58 us -> 5.77 us  [local(): arrived = [lax.ppermute(part, 'tchunk', swap) for part in theirs]]
    ppermute x2 -> x1, starting transfers between devices: 5.28 us -> 1.92 us  [local(): arrived = [lax.ppermute(part, 'tchunk', swap) for part in theirs]]
    pallas_call x2 -> x1, Pallas kernels: 1.5 us -> 0.87 us  [add_parts(): pl.pallas_call(add_rows, out_shape=jax.ShapeDtypeStruct((2, rows, columns...]
  transfers between devices with their start and end apart: 3 -> 2, of which waited for: 3 -> 2; matrix products, arithmetic and copies ran while one was open for 0% -> 0% of each run, Pallas kernels for 2% -> 1%
where the time goes in v6:
time: 49.2 us; the launch traced here: 48.6 us
  waiting for transfers between devices  25.5 us (52%)
  starting transfers between devices  18.4 us (37%)
  Pallas kernels  4.69 us (10%)
    all_to_all x1, waiting for transfers between devices, local(): lax.all_to_all(formed, ('stn', 'tchunk'), 0, 0, axis_index_groups=classes...  19.8 us
    all_to_all x1, starting transfers between devices, local(): lax.all_to_all(formed, ('stn', 'tchunk'), 0, 0, axis_index_groups=classes...  16.5 us
    ppermute x1, waiting for transfers between devices, local(): arrived = [lax.ppermute(part, 'tchunk', swap) for part in theirs]  5.77 us
    pallas_call x1, Pallas kernels, local(): pl.pallas_call(lambda *refs: form_beams(times // 2, pieces, *refs), out_s...  3.13 us
    ppermute x1, starting transfers between devices, local(): arrived = [lax.ppermute(part, 'tchunk', swap) for part in theirs]  1.92 us
  transfers between devices with their start and end apart: 2, of which 2 were waited for; matrix products, arithmetic and copies ran while one was open for 0% of the time, Pallas kernels for 1%

profile of v6, /device:TPU:1, one launch (start us, length us, event | category | flops | bytes accessed | tf_op | source)
XLA Modules:
  0.0 48.6 jit_solution(16571353090152260044)
XLA Ops:
  0.0 3.1 %form_beams.1 = bf16[32,2,2,16,128]{4,3,2,1,0:T(8,128)(2,1)} custom-call(bf16[16,128,512]{2,1,0:T(8,128)(2,1)} %bitcast.10, bf16[16,2,32,256]{3,2,1,0:T(8,128)(2,1)} %bitcast.11), custom_call_target="tpu_custom_call" | custom-call | tf_op jit(solution)/shard_map/form_beams/pallas_call | solution.py:145
  3.1 16.5 %all-to-all-start = ((bf16[64,2,16,128]{3,2,1,0:T(8,128)(2,1)}), bf16[64,2,16,128]{3,2,1,0:T(8,128)(2,1)S(1)}, u32[]{:S(2)}, u32[]{:S(2)}) async-start(bf16[64,2,16,128]{3,2,1,0:T(8,128)(2,1)} %bitcast.3), calls=%async_computation | async-start | bytes 1048576 | tf_op jit(solution)/shard_map/all_to_all | solution.py:164
  19.6 19.8 %all-to-all-done = bf16[64,2,16,128]{3,2,1,0:T(8,128)(2,1)S(1)} async-done(((bf16[64,2,16,128]{3,2,1,0:T(8,128)(2,1)}), bf16[64,2,16,128]{3,2,1,0:T(8,128)(2,1)S(1)}, u32[]{:S(2)}, u32[]{:S(2)}) %all-to-all-start) | async-done | bytes 524320 | tf_op jit(solution)/shard_map/all_to_all | solution.py:164
  39.4 0.3 correlate_theirs.1
  39.7 1.9 %collective-permute-start = (bf16[128,896]{1,0:T(8,128)(2,1)S(1)}, bf16[128,896]{1,0:T(8,128)(2,1)S(1)}, u32[]{:S(2)}, u32[]{:S(2)}) collective-permute-start(bf16[128,896]{1,0:T(8,128)(2,1)S(1)} %correlate_theirs.1), channel_id=1, source_target_pairs={{0,1},{1,0},{2,3},{3,2},{4,5},{5,4},{6,7},{7,6},{8,9},{9,8},{10,11... | collective-permute-start | bytes 688136 | tf_op jit(solution)/shard_map/ppermute | solution.py:172
  41.6 0.4 correlate_ours.1
  42.0 5.8 %collective-permute-done.refs_0_ = bf16[128,896]{1,0:T(8,128)(2,1)S(1)} collective-permute-done((bf16[128,896]{1,0:T(8,128)(2,1)S(1)}, bf16[128,896]{1,0:T(8,128)(2,1)S(1)}, u32[]{:S(2)}, u32[]{:S(2)}) %collective-permute-start) | collective-permute-done | bytes 229408 | tf_op jit(solution)/shard_map/ppermute | solution.py:172
  47.8 0.9 %add_parts.1 = f32[2,128,512]{2,1,0:T(8,128)} custom-call(s32[1]{0:T(128)} %bitcast.refs_0_.row_ref, f32[128,512]{1,0:T(8,128)S(1)} %get-tuple-element.7.re_ref, f32[128,512]{1,0:T(8,128)S(1)} %get-tuple-element.8.im_ref, bf16[128,896]{1,0:T(8,128)(2,1)S(1)} %collective-permute-done.refs_0_), custom_call_target="tpu_custom_call" | custom-call | flops 65536 | bytes 524288 | tf_op jit(solution)/shard_map/add_parts/pallas_call | solution.py:126
Async XLA Ops:
  3.1 36.2 %all-to-all-start = ((bf16[64,2,16,128]{3,2,1,0:T(8,128)(2,1)}), bf16[64,2,16,128]{3,2,1,0:T(8,128)(2,1)S(1)}, u32[]{:S(2)}, u32[]{:S(2)}) async-start(bf16[64,2,16,128]{3,2,1,0:T(8,128)(2,1)} %bitcast.3), calls=%async_computation | async-start | bytes 1048576 | tf_op jit(solution)/shard_map/all_to_all | solution.py:164
  39.7 8.1 %collective-permute-start = (bf16[128,896]{1,0:T(8,128)(2,1)S(1)}, bf16[128,896]{1,0:T(8,128)(2,1)S(1)}, u32[]{:S(2)}, u32[]{:S(2)}) collective-permute-start(bf16[128,896]{1,0:T(8,128)(2,1)S(1)} %correlate_theirs.1), channel_id=1, source_target_pairs={{0,1},{1,0},{2,3},{3,2},{4,5},{5,4},{6,7},{7,6},{8,9},{9,8},{10,11... | collective-permute-start | bytes 688136 | tf_op jit(solution)/shard_map/ppermute | solution.py:172

commit v7 on v6

--- a/solution.py
+++ b/solution.py
@@ -23,17 +23,21 @@
     for pair in loads:
         for load in pair:
             load.start()
-    for s in range(stations):
+    for s in range(0, stations, 2):
         if s % step == 0:
             for load in loads[s // step]:
                 load.wait()
-        w_re = wgt_ref[s, 0]
-        w_im = wgt_ref[s, 1]
-        upper = jnp.concatenate([w_re, -w_im], axis=-1)
-        lower = jnp.concatenate([w_im, w_re], axis=-1)
-        matrix = jnp.concatenate([upper, lower], axis=0)
-        formed = lax.dot_general(matrix, volt_ref[s], NT_DIMS, preferred_element_type=jnp.float32)
-        held[s] = formed.reshape(held.shape[1:])
+        matrices = []
+        for q in (s, s + 1):
+            w_re = wgt_ref[q, 0]
+            w_im = wgt_ref[q, 1]
+            matrices += [jnp.concatenate([w_re, -w_im], axis=-1), jnp.concatenate([w_im, w_re], axis=-1)]
+        samples = volt_ref.shape[1]
+        both = volt_ref[s : s + 2].reshape(2 * samples, volt_ref.shape[2])
+        formed = lax.dot_general(jnp.concatenate(matrices, axis=0), both, NT_DIMS, preferred_element_type=jnp.float32)
+        half = formed.shape[0] // 2
+        held[s] = formed[:half, :samples].reshape(held.shape[1:])
+        held[s + 1] = formed[half:, samples:].reshape(held.shape[1:])
     rounded = jnp.transpose(held[...], (2, 1, 0, 3)).astype(jnp.bfloat16)
     for b in range(beam_count):
         for c in range(copies):

time: 49.2 us -> 49.2 us (level)
  no operation moved by 1% of the time
where the time goes in v7:
time: 49.2 us; the launch traced here: 48.6 us
  waiting for transfers between devices  25.5 us (52%)
  starting transfers between devices  18.4 us (37%)
  Pallas kernels  4.7 us (10%)
    all_to_all x1, waiting for transfers between devices, local(): lax.all_to_all(formed, ('stn', 'tchunk'), 0, 0, axis_index_groups=classes...  19.8 us
    all_to_all x1, starting transfers between devices, local(): lax.all_to_all(formed, ('stn', 'tchunk'), 0, 0, axis_index_groups=classes...  16.4 us
    ppermute x1, waiting for transfers between devices, local(): arrived = [lax.ppermute(part, 'tchunk', swap) for part in theirs]  5.77 us
    pallas_call x1, Pallas kernels, local(): pl.pallas_call(lambda *refs: form_beams(times // 2, pieces, *refs), out_s...  3.14 us
    ppermute x1, starting transfers between devices, local(): arrived = [lax.ppermute(part, 'tchunk', swap) for part in theirs]  1.92 us
  transfers between devices with their start and end apart: 2, of which 2 were waited for; matrix products, arithmetic and copies ran while one was open for 0% of the time, Pallas kernels for 1%

profile of v7, /device:TPU:1, one launch (start us, length us, event | category | flops | bytes accessed | tf_op | source)
XLA Modules:
  0.0 48.6 jit_solution(2984114171844253409)
XLA Ops:
  0.0 3.1 %form_beams.1 = bf16[32,2,2,16,128]{4,3,2,1,0:T(8,128)(2,1)} custom-call(bf16[16,128,512]{2,1,0:T(8,128)(2,1)} %bitcast.10, bf16[16,2,32,256]{3,2,1,0:T(8,128)(2,1)} %bitcast.11), custom_call_target="tpu_custom_call" | custom-call | tf_op jit(solution)/shard_map/form_beams/pallas_call | solution.py:149
  3.1 16.4 %all-to-all-start = ((bf16[64,2,16,128]{3,2,1,0:T(8,128)(2,1)}), bf16[64,2,16,128]{3,2,1,0:T(8,128)(2,1)S(1)}, u32[]{:S(2)}, u32[]{:S(2)}) async-start(bf16[64,2,16,128]{3,2,1,0:T(8,128)(2,1)} %bitcast.3), calls=%async_computation | async-start | bytes 1048576 | tf_op jit(solution)/shard_map/all_to_all | solution.py:168
  19.6 19.8 %all-to-all-done = bf16[64,2,16,128]{3,2,1,0:T(8,128)(2,1)S(1)} async-done(((bf16[64,2,16,128]{3,2,1,0:T(8,128)(2,1)}), bf16[64,2,16,128]{3,2,1,0:T(8,128)(2,1)S(1)}, u32[]{:S(2)}, u32[]{:S(2)}) %all-to-all-start) | async-done | bytes 524320 | tf_op jit(solution)/shard_map/all_to_all | solution.py:168
  39.4 0.3 correlate_theirs.1
  39.7 1.9 %collective-permute-start = (bf16[128,896]{1,0:T(8,128)(2,1)S(1)}, bf16[128,896]{1,0:T(8,128)(2,1)S(1)}, u32[]{:S(2)}, u32[]{:S(2)}) collective-permute-start(bf16[128,896]{1,0:T(8,128)(2,1)S(1)} %correlate_theirs.1), channel_id=1, source_target_pairs={{0,1},{1,0},{2,3},{3,2},{4,5},{5,4},{6,7},{7,6},{8,9},{9,8},{10,11... | collective-permute-start | bytes 688136 | tf_op jit(solution)/shard_map/ppermute | solution.py:176
  41.6 0.4 correlate_ours.1
  42.0 5.8 %collective-permute-done.refs_0_ = bf16[128,896]{1,0:T(8,128)(2,1)S(1)} collective-permute-done((bf16[128,896]{1,0:T(8,128)(2,1)S(1)}, bf16[128,896]{1,0:T(8,128)(2,1)S(1)}, u32[]{:S(2)}, u32[]{:S(2)}) %collective-permute-start) | collective-permute-done | bytes 229408 | tf_op jit(solution)/shard_map/ppermute | solution.py:176
  47.8 0.9 %add_parts.1 = f32[2,128,512]{2,1,0:T(8,128)} custom-call(s32[1]{0:T(128)} %bitcast.refs_0_.row_ref, f32[128,512]{1,0:T(8,128)S(1)} %get-tuple-element.7.re_ref, f32[128,512]{1,0:T(8,128)S(1)} %get-tuple-element.8.im_ref, bf16[128,896]{1,0:T(8,128)(2,1)S(1)} %collective-permute-done.refs_0_), custom_call_target="tpu_custom_call" | custom-call | flops 65536 | bytes 524288 | tf_op jit(solution)/shard_map/add_parts/pallas_call | solution.py:130
Async XLA Ops:
  3.1 36.2 %all-to-all-start = ((bf16[64,2,16,128]{3,2,1,0:T(8,128)(2,1)}), bf16[64,2,16,128]{3,2,1,0:T(8,128)(2,1)S(1)}, u32[]{:S(2)}, u32[]{:S(2)}) async-start(bf16[64,2,16,128]{3,2,1,0:T(8,128)(2,1)} %bitcast.3), calls=%async_computation | async-start | bytes 1048576 | tf_op jit(solution)/shard_map/all_to_all | solution.py:168
  39.7 8.1 %collective-permute-start = (bf16[128,896]{1,0:T(8,128)(2,1)S(1)}, bf16[128,896]{1,0:T(8,128)(2,1)S(1)}, u32[]{:S(2)}, u32[]{:S(2)}) collective-permute-start(bf16[128,896]{1,0:T(8,128)(2,1)S(1)} %correlate_theirs.1), channel_id=1, source_target_pairs={{0,1},{1,0},{2,3},{3,2},{4,5},{5,4},{6,7},{7,6},{8,9},{9,8},{10,11... | collective-permute-start | bytes 688136 | tf_op jit(solution)/shard_map/ppermute | solution.py:176

commit v8 on v5

--- a/solution.py
+++ b/solution.py
@@ -24,17 +24,21 @@
     for pair in loads:
         for load in pair:
             load.start()
-    for s in range(stations):
+    for s in range(0, stations, 2):
         if s % step == 0:
             for load in loads[s // step]:
                 load.wait()
-        w_re = wgt_ref[s, 0]
-        w_im = wgt_ref[s, 1]
-        upper = jnp.concatenate([w_re, -w_im], axis=-1)
-        lower = jnp.concatenate([w_im, w_re], axis=-1)
-        matrix = jnp.concatenate([upper, lower], axis=0)
-        formed = lax.dot_general(matrix, volt_ref[s], NT_DIMS, preferred_element_type=jnp.float32)
-        held[s] = formed.reshape(held.shape[1:])
+        matrices = []
+        for q in (s, s + 1):
+            w_re = wgt_ref[q, 0]
+            w_im = wgt_ref[q, 1]
+            matrices += [jnp.concatenate([w_re, -w_im], axis=-1), jnp.concatenate([w_im, w_re], axis=-1)]
+        samples = volt_ref.shape[1]
+        both = volt_ref[s : s + 2].reshape(2 * samples, volt_ref.shape[2])
+        formed = lax.dot_general(jnp.concatenate(matrices, axis=0), both, NT_DIMS, preferred_element_type=jnp.float32)
+        half = formed.shape[0] // 2
+        held[s] = formed[:half, :samples].reshape(held.shape[1:])
+        held[s + 1] = formed[half:, samples:].reshape(held.shape[1:])
     rounded = jnp.transpose(held[...], (2, 1, 0, 3)).astype(jnp.bfloat16)
     for b in range(beam_count):
         for c in range(copies):

time: 49 us -> 49 us (level)
  no operation moved by 1% of the time
where the time goes in v8:
time: 49 us; the launch traced here: 48.5 us
  starting transfers between devices  21.7 us (44%)
  waiting for transfers between devices  21.3 us (43%)
  Pallas kernels  5.33 us (11%)
    all_to_all x1, waiting for transfers between devices, local(): lax.all_to_all(formed, ('stn', 'tchunk'), 0, 0, axis_index_groups=classes...  19.8 us
    all_to_all x1, starting transfers between devices, local(): lax.all_to_all(formed, ('stn', 'tchunk'), 0, 0, axis_index_groups=classes...  16.4 us
    ppermute x2, starting transfers between devices, local(): arrived = [lax.ppermute(part, 'tchunk', swap) for part in theirs]  5.28 us
    pallas_call x1, Pallas kernels, local(): pl.pallas_call(lambda *refs: form_beams(times // 2, pieces, *refs), out_s...  3.14 us
    ppermute x2, waiting for transfers between devices, local(): arrived = [lax.ppermute(part, 'tchunk', swap) for part in theirs]  1.58 us
    pallas_call x2, Pallas kernels, add_part(): pl.pallas_call(lambda *refs: add_rows(stage, *refs), out_shape=jax.ShapeD...  1.5 us
  transfers between devices with their start and end apart: 3, of which 3 were waited for; matrix products, arithmetic and copies ran while one was open for 0% of the time, Pallas kernels for 2%

profile of v8, /device:TPU:1, one launch (start us, length us, event | category | flops | bytes accessed | tf_op | source)
XLA Modules:
  0.0 48.5 jit_solution(9713210335912081399)
XLA Ops:
  0.0 3.1 %form_beams.1 = bf16[32,2,2,16,128]{4,3,2,1,0:T(8,128)(2,1)} custom-call(bf16[16,128,512]{2,1,0:T(8,128)(2,1)} %bitcast.10, bf16[16,2,32,256]{3,2,1,0:T(8,128)(2,1)} %bitcast.11), custom_call_target="tpu_custom_call" | custom-call | tf_op jit(solution)/shard_map/form_beams/pallas_call | solution.py:153
  3.1 16.4 %all-to-all-start = ((bf16[64,2,16,128]{3,2,1,0:T(8,128)(2,1)}), bf16[64,2,16,128]{3,2,1,0:T(8,128)(2,1)S(1)}, u32[]{:S(2)}, u32[]{:S(2)}) async-start(bf16[64,2,16,128]{3,2,1,0:T(8,128)(2,1)} %bitcast.3), calls=%async_computation | async-start | bytes 1048576 | tf_op jit(solution)/shard_map/all_to_all | solution.py:172
  19.6 19.8 %all-to-all-done = bf16[64,2,16,128]{3,2,1,0:T(8,128)(2,1)S(1)} async-done(((bf16[64,2,16,128]{3,2,1,0:T(8,128)(2,1)}), bf16[64,2,16,128]{3,2,1,0:T(8,128)(2,1)S(1)}, u32[]{:S(2)}, u32[]{:S(2)}) %all-to-all-start) | async-done | bytes 524320 | tf_op jit(solution)/shard_map/all_to_all | solution.py:172
  39.4 0.3 correlate_theirs.1
  39.7 1.9 %collective-permute-start.1 = (bf16[128,640]{1,0:T(8,128)(2,1)S(1)}, bf16[128,640]{1,0:T(8,128)(2,1)S(1)}, u32[]{:S(2)}, u32[]{:S(2)}) collective-permute-start(bf16[128,640]{1,0:T(8,128)(2,1)S(1)} %get-tuple-element.12), channel_id=1, source_target_pairs={{0,1},{1,0},{2,3},{3,2},{4,5},{5,4},{6,7},{7,6},{8,9},{9,8},{10,11... | collective-permute-start | bytes 491528 | tf_op jit(solution)/shard_map/ppermute | solution.py:180
  41.6 3.4 %collective-permute-start = (bf16[128,256]{1,0:T(8,128)(2,1)S(1)}, bf16[128,256]{1,0:T(8,128)(2,1)S(1)}, u32[]{:S(2)}, u32[]{:S(2)}) collective-permute-start(bf16[128,256]{1,0:T(8,128)(2,1)S(1)} %get-tuple-element.11), channel_id=1, source_target_pairs={{0,1},{1,0},{2,3},{3,2},{4,5},{5,4},{6,7},{7,6},{8,9},{9,8},{10,11... | collective-permute-start | bytes 196616 | tf_op jit(solution)/shard_map/ppermute | solution.py:180
  45.0 0.4 correlate_ours.1
  45.4 1.0 %collective-permute-done.1.refs_3_ = bf16[128,640]{1,0:T(8,128)(2,1)S(1)} collective-permute-done((bf16[128,640]{1,0:T(8,128)(2,1)S(1)}, bf16[128,640]{1,0:T(8,128)(2,1)S(1)}, u32[]{:S(2)}, u32[]{:S(2)}) %collective-permute-start.1) | collective-permute-done | bytes 163872 | tf_op jit(solution)/shard_map/ppermute | solution.py:180
  46.4 0.8 %add_first.1.refs_4_ = f32[2,128,512]{2,1,0:T(8,128)} custom-call(s32[1]{0:T(128)} %bitcast.refs_0_, f32[128,512]{1,0:T(8,128)S(1)} %get-tuple-element.9.refs_1_, f32[128,512]{1,0:T(8,128)S(1)} %get-tuple-element.10.refs_2_, bf16[128,640]{1,0:T(8,128)(2,1)S(1)} %collective-permute-done.1.refs_3_), custom_call_target="tpu_custom_call" | custom-call | flops 65536 | bytes 524288 | tf_op jit(solution)/shard_map/add_first/pallas_call | solution.py:133
  47.2 0.6 %collective-permute-done.refs_3_ = bf16[128,256]{1,0:T(8,128)(2,1)S(1)} collective-permute-done((bf16[128,256]{1,0:T(8,128)(2,1)S(1)}, bf16[128,256]{1,0:T(8,128)(2,1)S(1)}, u32[]{:S(2)}, u32[]{:S(2)}) %collective-permute-start) | collective-permute-done | bytes 65568 | tf_op jit(solution)/shard_map/ppermute | solution.py:180
  47.8 0.7 %add_last.1 = f32[2,128,512]{2,1,0:T(8,128)} custom-call(s32[1]{0:T(128)} %bitcast.refs_0_, f32[128,512]{1,0:T(8,128)S(1)} %get-tuple-element.9.refs_1_, f32[128,512]{1,0:T(8,128)S(1)} %get-tuple-element.10.refs_2_, bf16[128,256]{1,0:T(8,128)(2,1)S(1)} %collective-permute-done.refs_3_, f32[2,128,512]{2,1,0:T(8,128)} %add_first.1.refs_4_), custom_call_target="tpu_custom_call", output_to_operand_aliasing={{}: (4, {})} | custom-call | flops 65536 | bytes 524288 | tf_op jit(solution)/shard_map/add_last/pallas_call | solution.py:133
Async XLA Ops:
  3.1 36.2 %all-to-all-start = ((bf16[64,2,16,128]{3,2,1,0:T(8,128)(2,1)}), bf16[64,2,16,128]{3,2,1,0:T(8,128)(2,1)S(1)}, u32[]{:S(2)}, u32[]{:S(2)}) async-start(bf16[64,2,16,128]{3,2,1,0:T(8,128)(2,1)} %bitcast.3), calls=%async_computation | async-start | bytes 1048576 | tf_op jit(solution)/shard_map/all_to_all | solution.py:172
  39.7 6.7 %collective-permute-start.1 = (bf16[128,640]{1,0:T(8,128)(2,1)S(1)}, bf16[128,640]{1,0:T(8,128)(2,1)S(1)}, u32[]{:S(2)}, u32[]{:S(2)}) collective-permute-start(bf16[128,640]{1,0:T(8,128)(2,1)S(1)} %get-tuple-element.12), channel_id=1, source_target_pairs={{0,1},{1,0},{2,3},{3,2},{4,5},{5,4},{6,7},{7,6},{8,9},{9,8},{10,11... | collective-permute-start | bytes 491528 | tf_op jit(solution)/shard_map/ppermute | solution.py:180
  41.6 6.1 %collective-permute-start = (bf16[128,256]{1,0:T(8,128)(2,1)S(1)}, bf16[128,256]{1,0:T(8,128)(2,1)S(1)}, u32[]{:S(2)}, u32[]{:S(2)}) collective-permute-start(bf16[128,256]{1,0:T(8,128)(2,1)S(1)} %get-tuple-element.11), channel_id=1, source_target_pairs={{0,1},{1,0},{2,3},{3,2},{4,5},{5,4},{6,7},{7,6},{8,9},{9,8},{10,11... | collective-permute-start | bytes 196616 | tf_op jit(solution)/shard_map/ppermute | solution.py:180
